TPU v7x, 128 devices: a whole 4x4x4 slice. The times are simulated.
128 devices in a mesh: freq: 4 (over y), sky: 32 (over x, z, core).
Axes of the slice: x: 4, y: 4, z: 4, core: 2. Of those that a mesh axis runs over, the one named last changes fastest.
Arguments:
- stokes: bfloat16 [2, 288, 128, 1024], P(None, 'freq', 'sky'), may hold values from -48 to 48
- lam2: float32 [288], replicated, may hold values from 0.02 to 0.14
- peaks: int32 [8, 128, 1024], P(None, 'sky'), may hold values from 0 to 2047
- island_owner: int32 [1024, 1], P('sky'), may hold values from 0 to 31; in each aligned block of 32 rows (0 to 31, 32 to 63, ...) at most 2 rows name the same one
- fit_matrix: bfloat16 [32, 576, 512], P('sky', None, 'freq'), may hold values from -0.03125 to 0.03125
Outputs:
- residual_fdf: bfloat16 [2, 2048, 128, 1024], P(None, 'freq', 'sky')
- fit_coeffs: float32 [32, 32, 2, 128, 512], P('sky', None, None, None, 'freq')
Inputs may be any that keep to these rules, and one draw needn't show every extreme that they name: `island_owner`: among the 32 blocks of one index of sky, no owner is named more than 2 times.
All inputs are finite; a program needn't handle non-finite values.
Results may differ from a plain program's by a relative error of at most 0.0065.
Values may be sent and summed in bfloat16 or wider, within the bound.
A program may use at most 192 MiB of HBM per device.

v0:
```python
import functools
import jax
import jax.numpy as jnp
from jax import lax
from jax.sharding import PartitionSpec as P
from jax.experimental import pallas as pl
from jax.experimental.pallas import tpu as pltpu

NC = 8
DEPTHS = 2048
STEP = 2.5
BLK = 128
GAIN = 0.3
LOW = 64
HIGH = 32

def gather(x, idx):
    return jnp.take_along_axis(x, idx, axis=1, mode="promise_in_bounds")

def full(row):
    return jnp.broadcast_to(row, (8, 128))

def clean_tile(groups, chans, data_ref, picks, t_ref, r_ref, out_ref, oh, e4, ec, es):
    lo = picks & (LOW - 1)
    hi = picks >> 6
    for j in range(NC):
        cols = slice(j * 128, (j + 1) * 128)
        low = (lax.broadcasted_iota(jnp.int32, (LOW, 128), 0) == lo[j:j+1]).astype(jnp.bfloat16)
        high = (lax.broadcasted_iota(jnp.int32, (HIGH, 128), 0) == hi[j:j+1]).astype(jnp.bfloat16)
        oh[0:LOW, cols] = low
        oh[LOW:2*LOW, cols] = low
        oh[2*LOW:2*LOW+HIGH, cols] = high
        oh[2*LOW+HIGH:, cols] = high
    e4[...] = jnp.dot(t_ref[...], oh[...], preferred_element_type=jnp.float32)

    def peak(g, acc):
        x = data_ref[pl.ds(pl.multiple_of(g * 16, 16), 16), :].astype(jnp.float32)
        q, u = x[:8], x[8:]
        base = pl.multiple_of(g * 32, 32)
        out = []
        for j in range(NC):
            cols = slice(j * 128, (j + 1) * 128)
            cl, sl = e4[pl.ds(base, 8), cols], e4[pl.ds(base + 8, 8), cols]
            ch, sh = e4[pl.ds(base + 16, 8), cols], e4[pl.ds(base + 24, 8), cols]
            c = ch * cl - sh * sl
            s = sh * cl + ch * sl
            ec[g * NC + j] = c
            es[g * NC + j] = s
            out.append((acc[j][0] + (q * c + u * s), acc[j][1] + (u * c - q * s)))
        return tuple(out)

    zero = jnp.zeros((8, 128), jnp.float32)
    acc = lax.fori_loop(0, groups, peak, tuple((zero, zero) for _ in range(NC)))
    scale = 1.0 / chans
    vr = jnp.concatenate([jnp.sum(a[0], axis=0, keepdims=True) for a in acc], axis=0) * scale
    vi = jnp.concatenate([jnp.sum(a[1], axis=0, keepdims=True) for a in acc], axis=0) * scale
    comps = []
    for i in range(NC):
        cr = full(vr[i:i+1] * GAIN)
        ci = full(vi[i:i+1] * GAIN)
        comps.append((cr, ci))
        if i == NC - 1:
            break
        d = picks - picks[i:i+1]
        a = jnp.abs(d)
        alo, ahi = a & 127, a >> 7
        rr, ri = zero, zero
        for h in range(16):
            here = ahi == h
            rr = jnp.where(here, gather(full(r_ref[0, h:h+1, :]), alo), rr)
            ri = jnp.where(here, gather(full(r_ref[1, h:h+1, :]), alo), ri)
        ri = jnp.where(d < 0, -ri, ri)
        vr = vr - (cr * rr - ci * ri)
        vi = vi - (cr * ri + ci * rr)

    def model(g, _):
        rows16 = pl.ds(pl.multiple_of(g * 16, 16), 16)
        x = data_ref[rows16, :].astype(jnp.float32)
        mr, mi = zero, zero
        for j in range(NC):
            c, s = ec[g * NC + j], es[g * NC + j]
            cr, ci = comps[j]
            mr = mr + (cr * c - ci * s)
            mi = mi + (cr * s + ci * c)
        out_ref[rows16, :] = jnp.concatenate([x[:8] - mr, x[8:] - mi], axis=0).astype(jnp.bfloat16)
        return 0

    lax.fori_loop(0, groups, model, 0)

def kernel(groups, chans, data_ref, picks_ref, t_ref, r_ref, out_ref, oh, e4, ec, es):
    clean_tile(groups, chans, data_ref, picks_ref[...], t_ref, r_ref, out_ref, oh, e4, ec, es)

def clean(data, picks, t, r, chans):
    groups = chans // 8
    pixels = data.shape[1]
    return pl.pallas_call(
        functools.partial(kernel, groups, chans),
        grid=(pixels // 128,),
        in_specs=[
            pl.BlockSpec((2 * chans, 128), lambda i: (0, i)),
            pl.BlockSpec((NC, 128), lambda i: (0, i)),
            pl.BlockSpec((4 * chans, 2 * (LOW + HIGH)), lambda i: (0, 0)),
            pl.BlockSpec((2, 16, 128), lambda i: (0, 0, 0)),
        ],
        out_specs=pl.BlockSpec((2 * chans, 128), lambda i: (0, i)),
        out_shape=jax.ShapeDtypeStruct((2 * chans, pixels), jnp.bfloat16),
        scratch_shapes=[pltpu.VMEM((2 * (LOW + HIGH), 1024), jnp.bfloat16), pltpu.VMEM((4 * chans, 1024), jnp.float32)] + [pltpu.VMEM((groups * NC, 8, 128), jnp.float32)] * 2,
        compiler_params=pltpu.CompilerParams(vmem_limit_bytes=40 << 20),
        name="clean",
    )(data, picks, t, r)

def split(x):
    top = lax.reduce_precision(x, 8, 7)
    return top, x - top

def tables(lam2):
    chans = lam2.shape[0]
    off = lam2 - jnp.mean(lam2)
    a2 = 2.0 * off
    lo = a2[:, None] * (jnp.arange(LOW, dtype=jnp.float32) * 2.5)[None]
    hi = a2[:, None] * ((jnp.arange(HIGH, dtype=jnp.float32) * LOW - 1024.0) * 2.5)[None]
    def rows(a):
        return jnp.stack([jnp.cos(a), jnp.sin(a)]).reshape(2, chans // 8, 8, -1)
    l1, l2 = split(rows(lo)); h1, h2 = split(rows(hi))
    zl, zh = jnp.zeros_like(l1), jnp.zeros_like(h1)
    low = jnp.concatenate([l1, l2, zh, zh], -1)
    high = jnp.concatenate([zl, zl, h1, h2], -1)
    t = jnp.transpose(jnp.concatenate([low, high], 0), (1, 0, 2, 3)).reshape(4 * chans, -1)
    return off, t.astype(jnp.bfloat16)

def spread(off):
    a2 = 2.0 * off
    ah = (jnp.arange(16, dtype=jnp.float32) * 320.0)[:, None] * a2[None, :]
    ca, sa = jnp.cos(ah), jnp.sin(ah)
    al = a2[:, None] * (jnp.arange(128, dtype=jnp.float32) * 2.5)[None]
    left = jnp.stack([jnp.concatenate([ca, -sa], 1), jnp.concatenate([-sa, -ca], 1)])
    right = jnp.concatenate([jnp.cos(al), jnp.sin(al)], 0)
    return jnp.einsum("ahc,cl->ahl", left, right, precision=lax.Precision.HIGHEST) / off.shape[0]


def synthesis(off, first, count):
    chans = off.shape[0]
    per_row = jnp.broadcast_to(off.reshape(chans // 8, 1, 8), (chans // 8, 2, 8)).reshape(1, 2 * chans)
    is_u = (lax.broadcasted_iota(jnp.int32, (1, 2 * chans), 1) // 8) % 2 == 1
    depth = (jnp.arange(count) + first - DEPTHS // 2).astype(jnp.float32) * STEP
    angle = (2.0 * per_row) * depth[:, None]
    cosine, sine = jnp.cos(angle), jnp.sin(angle)
    real = jnp.where(is_u, sine, cosine)
    imag = jnp.where(is_u, cosine, -sine)
    return (jnp.concatenate([real, imag], axis=0) / chans).astype(jnp.bfloat16)


def fdf_kernel(k_ref, res_ref, out_ref, mixed):
    rows, depths, width = res_ref.shape[0], k_ref.shape[0], res_ref.shape[2]
    for row in range(rows):
        for first in range(0, depths, 256):
            part = jnp.dot(k_ref[first:first + 256, :], res_ref[row], preferred_element_type=jnp.float32)
            for c in range(width // 128):
                mixed[c, pl.ds(first * rows + row, 256, rows), :] = part[:, c * 128:(c + 1) * 128]
    for c in range(width // 128):
        block = mixed[c].astype(jnp.bfloat16)
        out_ref[:, :, :, c * 128:(c + 1) * 128] = block.reshape(2, depths // 2, rows, 128)


def fdf(kt, res):
    rows, total, columns = res.shape
    depths = kt.shape[0]
    width = 256
    return pl.pallas_call(
        fdf_kernel,
        grid=(columns // width,),
        in_specs=[
            pl.BlockSpec((depths, total), lambda i: (0, 0)),
            pl.BlockSpec((rows, total, width), lambda i: (0, 0, i)),
        ],
        out_specs=pl.BlockSpec((2, depths // 2, rows, width), lambda i: (0, 0, 0, i)),
        out_shape=jax.ShapeDtypeStruct((2, depths // 2, rows, columns), jnp.bfloat16),
        scratch_shapes=[pltpu.VMEM((width // 128, depths * rows, 128), jnp.float32)],
        compiler_params=pltpu.CompilerParams(vmem_limit_bytes=48 << 20),
        cost_estimate=pl.CostEstimate(flops=2 * depths * total * rows * columns, bytes_accessed=14 << 20, transcendentals=0),
        name="fdf",
    )(kt, res)


def slots_of(owners, count, capacity):
    blocks = owners.shape[0]
    index = jnp.arange(blocks)
    earlier = (owners[:, None] == owners[None, :]) & (index[None, :] < index[:, None])
    rank = jnp.sum(earlier.astype(jnp.int32), axis=1)
    hit = (owners[None, None, :] == jnp.arange(count)[:, None, None]) & (
        rank[None, None, :] == jnp.arange(capacity)[None, :, None])
    chosen = jnp.sum(jnp.where(hit, index[None, None, :], 0), axis=2).astype(jnp.int32)
    filled = jnp.sum(hit.astype(jnp.int32), axis=2)
    return chosen, filled


def fit_kernel(chosen, filled, *refs):
    capacity = len(refs) - 2
    w_ref, out_ref = refs[-2], refs[-1]
    owner = pl.program_id(0)
    for rank in range(capacity):
        value = lax.dot_general(refs[rank][0], w_ref[0], (((0,), (0,)), ((), ())), preferred_element_type=jnp.float32)
        out_ref[0, rank] = jnp.where(filled[owner, rank] > 0, value, 0.0).astype(jnp.bfloat16)


def fits(chosen, filled, res, w):
    count, capacity = chosen.shape
    rows, total, columns = res.shape
    per_row = columns // BLK
    terms = w.shape[2]

    def pick(rank):
        return pl.BlockSpec((1, total, BLK), lambda o, c, f: (c[o, rank] // per_row, 0, c[o, rank] % per_row))

    return pl.pallas_call(
        fit_kernel,
        grid_spec=pltpu.PrefetchScalarGridSpec(
            num_scalar_prefetch=2,
            grid=(count,),
            in_specs=[pick(rank) for rank in range(capacity)] + [pl.BlockSpec((1, total, terms), lambda o, c, f: (o, 0, 0))],
            out_specs=pl.BlockSpec((1, capacity, BLK, terms), lambda o, c, f: (o, 0, 0, 0)),
        ),
        out_shape=jax.ShapeDtypeStruct((count, capacity, BLK, terms), jnp.bfloat16),
        compiler_params=pltpu.CompilerParams(vmem_limit_bytes=32 << 20),
        name="fits",
    )(chosen, filled, *([res] * capacity), w)


def grouped(x, chans):
    tail = x.shape[2:]
    return jnp.swapaxes(x.reshape((2, chans // 8, 8) + tail), 0, 1)


def shards(stokes, lam2, peaks, island_owner, fit_matrix):
    freq = lax.axis_index("freq")
    freq_count, sky_count = lax.axis_size("freq"), lax.axis_size("sky")
    chans, local = lam2.shape[0], stokes.shape[1]
    rows, columns = stokes.shape[2], stokes.shape[3]
    capacity = max(2, 2 * island_owner.shape[0] // sky_count)
    weights = grouped(fit_matrix[0].reshape(2, chans, -1), chans).reshape(2 * chans, -1)
    weights = lax.all_gather(weights, "sky", axis=0)
    off, t = tables(lam2)
    outgoing = jnp.moveaxis(grouped(stokes, local), 3, 0).reshape(rows, 2 * local, columns)
    data = lax.all_to_all(outgoing, "freq", split_axis=0, concat_axis=0, tiled=True)
    picks = lax.dynamic_index_in_dim(peaks, freq, 1, keepdims=False)
    res = clean(data.reshape(2 * chans, columns), picks, t, spread(off), chans)
    res = lax.all_gather(res, "freq", axis=0)
    depths = DEPTHS // freq_count
    kt = synthesis(off, freq * depths, depths)
    chosen, filled = slots_of(island_owner[:, 0], sky_count, capacity)
    sent = fits(chosen, filled, res, weights)
    got = lax.all_to_all(sent, "sky", split_axis=0, concat_axis=0, tiled=True)
    return fdf(kt, res), got.astype(jnp.float32)[None]


def solution(mesh):
    in_specs = (
        P(None, "freq", "sky", None),
        P(),
        P(None, "sky", None),
        P("sky", None),
        P("sky", None, "freq"),
    )
    out_specs = (P(None, "freq", "sky", None), P("sky", None, None, None, "freq"))
    return jax.shard_map(shards, mesh=mesh, in_specs=in_specs, out_specs=out_specs, check_vma=False)
```

profile of v0, /device:TPU:1, one launch (start us, length us, event | category | flops | bytes accessed | tf_op | source)
XLA Modules:
  0.0 222.2 jit_solution(8893484864744944753)
XLA Ops:
  7.2 0.0 copy-start
  7.2 2.7 %copy.15 = bf16[4,9,2,8,1024]{4,3,2,1,0:T(8,128)(2,1)} copy(bf16[4,9,2,8,1024]{4,0,3,1,2:T(4,128)(2,1)} %bitcast.33) | data formatting | bytes 2359296 | tf_op jit(solution)/shard_map/transpose;transpose | solution.py:243
  9.9 0.0 copy-start.5
  9.9 5.1 %all-to-all-start = ((bf16[4,144,1024]{2,1,0:T(8,128)(2,1)}), bf16[4,144,1024]{2,1,0:T(8,128)(2,1)S(1)}, u32[]{:S(2)}, u32[]{:S(2)}) async-start(bf16[4,144,1024]{2,1,0:T(8,128)(2,1)} %bitcast.2), calls=%async_computation | async-start | bytes 2359296 | tf_op jit(solution)/shard_map/all_to_all | solution.py:244
  15.0 0.0 all-gather.6.cloned.1.call-start
  15.1 0.0 copy-done.5
  15.1 0.6 reduce_sum.36
  16.4 0.1 mul.173
  16.5 0.0 copy-done
  16.5 0.2 multiply_cosine_fusion.4
  16.7 0.6 multiply_cosine_fusion.1
  17.3 0.1 maximum_bitcast_fusion.2
  17.4 0.3 convolution_multiply_fusion.r_ref
  17.7 0.6 multiply_cosine_fusion.2
  18.3 0.1 reduce-precision_convert_fusion
  18.3 0.6 multiply_cosine_fusion.3
  18.9 0.1 reduce-precision_convert_fusion.1
  19.0 0.3 maximum_maximum_fusion
  19.3 11.3 %all-to-all-done = bf16[4,144,1024]{2,1,0:T(8,128)(2,1)S(1)} async-done(((bf16[4,144,1024]{2,1,0:T(8,128)(2,1)}), bf16[4,144,1024]{2,1,0:T(8,128)(2,1)S(1)}, u32[]{:S(2)}, u32[]{:S(2)}) %all-to-all-start) | async-done | bytes 1179680 | tf_op jit(solution)/shard_map/all_to_all | solution.py:244
  30.6 0.0 copy-start.4
  30.6 21.8 %clean.1 = bf16[576,1024]{1,0:T(8,128)(2,1)} custom-call(bf16[576,1024]{1,0:T(8,128)(2,1)S(1)} %bitcast.30, s32[8,1024]{1,0:T(8,128)S(1)} %bitcast.32, bf16[1152,192]{1,0:T(8,128)(2,1)S(1)} %bitcast.31, f32[2,16,128]{2,1,0:T(8,128)S(1)} %convolution_multiply_fusion.r_ref), custom_call_target="tpu_custom_call" | custom-call | tf_op jit(solution)/shard_map/clean/pallas_call | solution.py:96
  52.4 0.0 copy-start.6
  52.4 0.0 all-gather.6.cloned.1.call-update
  52.4 0.0 all-gather.4.cloned.1.call-start
  52.4 0.0 copy-done.4
  52.5 0.7 copy.17
  53.1 0.0 all-gather.4.cloned.1.call-update
  53.2 0.0 copy-done.6
  53.2 0.2 convert_reduce_fusion
  53.4 0.2 fusion.12
  53.5 0.1 copy.19.filled
  53.6 0.1 copy.18.chosen
  53.7 53.0 %all-gather.6.cloned.1.call-done = bf16[2304,1024]{1,0:T(8,128)(2,1)} async-done(((bf16[576,1024]{1,0:T(8,128)(2,1)}), bf16[2304,1024]{1,0:T(8,128)(2,1)}) %all-gather.6.cloned.1.call-update) | async-done | bytes 4718608 | tf_op jit(solution)/shard_map/all_gather | solution.py:247
  106.8 50.6 %all-gather.4.cloned.1.call-done.refs_2_ = bf16[32,576,128]{2,1,0:T(8,128)(2,1)} async-done(((bf16[1,576,128]{2,1,0:T(8,128)(2,1)}), bf16[32,576,128]{2,1,0:T(8,128)(2,1)}) %all-gather.4.cloned.1.call-update) | async-done | bytes 4718608 | tf_op jit(solution)/shard_map/all_gather | solution.py:241
  157.4 0.0 copy-start.1
  157.4 2.3 %copy-done.1 = bf16[2304,1024]{1,0:T(8,128)(2,1)S(1)} copy-done((bf16[2304,1024]{1,0:T(8,128)(2,1)S(1)}, bf16[2304,1024]{1,0:T(8,128)(2,1)}, u32[]{:S(2)}) %copy-start.1) | copy-done | bytes 4718616
  159.7 0.0 copy-start.3
  159.7 2.3 %copy-done.3 = bf16[32,576,128]{2,1,0:T(8,128)(2,1)S(1)} copy-done((bf16[32,576,128]{2,1,0:T(8,128)(2,1)S(1)}, bf16[32,576,128]{2,1,0:T(8,128)(2,1)}, u32[]{:S(2)}) %copy-start.3) | copy-done | bytes 4718616
  162.1 17.1 %fits.1 = bf16[32,2,128,128]{3,2,1,0:T(8,128)(2,1)} custom-call(s32[32,2]{1,0:T(8,128)S(1)} %copy.18.chosen, s32[32,2]{1,0:T(8,128)S(1)} %copy.19.filled, bf16[4,576,1024]{2,1,0:T(8,128)(2,1)S(1)} %bitcast.27, bf16[4,576,1024]{2,1,0:T(8,128)(2,1)S(1)} %bitcast.28, bf16[32,576,128]{2,1,0:T(8,128)(2,1)S(1)} %copy-done.3), custom_call_target="tpu_custom_call" | custom-call | tf_op jit(solution)/shard_map/fits/pallas_call | solution.py:215
  179.2 5.3 %all-to-all-start.1 = ((bf16[32,2,128,128]{3,2,1,0:T(8,128)(2,1)}), bf16[32,2,128,128]{3,2,1,0:T(8,128)(2,1)S(1)}, u32[]{:S(2)}, u32[]{:S(2)}) async-start(bf16[32,2,128,128]{3,2,1,0:T(8,128)(2,1)} %fits.1), calls=%async_computation.1 | async-start | bytes 4194304 | tf_op jit(solution)/shard_map/all_to_all | solution.py:252
  184.6 0.1 mul.174
  184.7 0.0 copy-start.2
  184.7 4.7 %fusion.2 = (f32[512,576]{1,0:T(8,128)S(1)}, f32[512,576]{1,0:T(8,128)S(1)}) fusion(f32[512]{0:T(512)S(1)} %convert_multiply_fusion, f32[576]{0:T(1024)S(1)} %mul.174, pred[576]{0:T(1024)(128)(4,1)S(1)} %fusion.17), kind=kLoop, calls=%fused_computation.6 | loop fusion | flops 1179648 | bytes 2364224 | tf_op jit(solution)/shard_map/jit(_where)/select_n | solution.py:148
  189.4 0.3 fusion.k_ref
  189.7 0.0 copy-done.2
  189.7 11.7 %fdf.1 = bf16[2,512,4,1024]{3,2,1,0:T(4,128)(2,1)} custom-call(bf16[1024,576]{1,0:T(8,128)(2,1)S(1)} %fusion.k_ref, bf16[4,576,1024]{2,1,0:T(8,128)(2,1)S(1)} %bitcast.29), custom_call_target="tpu_custom_call" | custom-call | flops 4831838208 | bytes 14680064 | tf_op jit(solution)/shard_map/fdf/pallas_call | solution.py:169
  201.4 11.4 %all-to-all-done.1 = bf16[32,2,128,128]{3,2,1,0:T(8,128)(2,1)S(1)} async-done(((bf16[32,2,128,128]{3,2,1,0:T(8,128)(2,1)}), bf16[32,2,128,128]{3,2,1,0:T(8,128)(2,1)S(1)}, u32[]{:S(2)}, u32[]{:S(2)}) %all-to-all-start.1) | async-done | bytes 2097184 | tf_op jit(solution)/shard_map/all_to_all | solution.py:252
  212.8 2.5 %bitcast_convert_fusion = f32[1,32,2,128,128]{4,3,2,1,0:T(8,128)} fusion(bf16[32,2,128,128]{3,2,1,0:T(8,128)(2,1)S(1)} %all-to-all-done.1), kind=kLoop, calls=%fused_computation.2 | loop fusion | flops 1048576 | bytes 6291456 | tf_op jit(solution)/shard_map/broadcast_in_dim | solution.py:253
  (16 shorter events, 0.2 us)
Async XLA Ops:
  7.2 9.3 %copy-start = (s32[8,4,1024]{2,1,0:T(4,128)S(1)}, s32[8,4,1024]{2,1,0:T(4,128)}, u32[]{:S(2)}) copy-start(s32[8,4,1024]{2,1,0:T(4,128)} %param.7) | copy-start | bytes 393220
  9.9 5.2 %copy-start.5 = (f32[288]{0:T(512)S(1)}, f32[288]{0:T(512)}, u32[]{:S(2)}) copy-start(f32[288]{0:T(512)} %param.6) | copy-start | bytes 3460
  9.9 20.7 %all-to-all-start = ((bf16[4,144,1024]{2,1,0:T(8,128)(2,1)}), bf16[4,144,1024]{2,1,0:T(8,128)(2,1)S(1)}, u32[]{:S(2)}, u32[]{:S(2)}) async-start(bf16[4,144,1024]{2,1,0:T(8,128)(2,1)} %bitcast.2), calls=%async_computation | async-start | bytes 2359296 | tf_op jit(solution)/shard_map/all_to_all | solution.py:244
  15.0 91.8 %all-gather.6.cloned.1.call-start = ((), (), s32[]{:S(2)}) async-start(), calls=%async_computation.3 | async-start | bytes 5898240 | tf_op jit(solution)/shard_map/all_gather | solution.py:247
  30.6 21.9 %copy-start.4 = (bf16[1,576,128]{2,1,0:T(8,128)(2,1)S(1)}, bf16[1,576,128]{2,1,0:T(8,128)(2,1)}, u32[]{:S(2)}) copy-start(bf16[1,576,128]{2,1,0:T(8,128)(2,1)} %param.9) | copy-start | bytes 442372
  52.4 0.8 copy-start.6
  52.4 105.0 %all-gather.4.cloned.1.call-start = ((), (), s32[]{:S(2)}) async-start(), calls=%async_computation.2 | async-start | bytes 4866048 | tf_op jit(solution)/shard_map/all_gather | solution.py:241
  157.4 2.3 %copy-start.1 = (bf16[2304,1024]{1,0:T(8,128)(2,1)S(1)}, bf16[2304,1024]{1,0:T(8,128)(2,1)}, u32[]{:S(2)}) copy-start(bf16[2304,1024]{1,0:T(8,128)(2,1)} %all-gather.6.cloned.1.call-done) | copy-start | bytes 14155780
  159.7 2.3 %copy-start.3 = (bf16[32,576,128]{2,1,0:T(8,128)(2,1)S(1)}, bf16[32,576,128]{2,1,0:T(8,128)(2,1)}, u32[]{:S(2)}) copy-start(bf16[32,576,128]{2,1,0:T(8,128)(2,1)} %all-gather.4.cloned.1.call-done.refs_2_) | copy-start | bytes 14155780
  179.2 33.6 %all-to-all-start.1 = ((bf16[32,2,128,128]{3,2,1,0:T(8,128)(2,1)}), bf16[32,2,128,128]{3,2,1,0:T(8,128)(2,1)S(1)}, u32[]{:S(2)}, u32[]{:S(2)}) async-start(bf16[32,2,128,128]{3,2,1,0:T(8,128)(2,1)} %fits.1), calls=%async_computation.1 | async-start | bytes 4194304 | tf_op jit(solution)/shard_map/all_to_all | solution.py:252
  184.7 5.0 %copy-start.2 = (bf16[2304,1024]{1,0:T(8,128)(2,1)S(1)}, bf16[2304,1024]{1,0:T(8,128)(2,1)}, u32[]{:S(2)}) copy-start(bf16[2304,1024]{1,0:T(8,128)(2,1)} %all-gather.6.cloned.1.call-done) | copy-start | bytes 14155780
Sparse Core Ops, SparseCore 0:
  52.5 54.1 all-gather.5
  109.6 47.7 all-gather.3
where the time goes:
time: 223 us; the launch traced here: 222 us
  waiting for transfers between devices  126 us (57%)
  Pallas kernels  50.6 us (23%)
  between operations  14.9 us (7%)
  other arithmetic  10.9 us (5%)
  starting transfers between devices  10.5 us (5%)
  local copies, waits for them, and re-layouts  8.5 us (4%)
    all_gather x1, waiting for transfers between devices, shards(): res = lax.all_gather(res, 'freq', axis=0)  53 us
    all_gather x1, waiting for transfers between devices, shards(): weights = lax.all_gather(weights, 'sky', axis=0)  50.6 us
    pallas_call x1, Pallas kernels, clean(): pl.pallas_call(functools.partial(kernel, groups, chans), grid=(pixels //...  21.8 us
    pallas_call x1, Pallas kernels, fits(): pl.pallas_call(fit_kernel, grid_spec=pltpu.PrefetchScalarGridSpec(num_sca...  17.1 us
    pallas_call x1, Pallas kernels, fdf(): pl.pallas_call(fdf_kernel, grid=(columns // width,), in_specs=[pl.BlockSp...  11.7 us
    all_to_all x1, waiting for transfers between devices, shards(): got = lax.all_to_all(sent, 'sky', split_axis=0, concat_axis=0, tiled=True)  11.4 us
    all_to_all x1, waiting for transfers between devices, shards(): lax.all_to_all(outgoing, 'freq', split_axis=0, concat_axis=0, tiled=True)  11.3 us
    all_to_all x1, starting transfers between devices, shards(): got = lax.all_to_all(sent, 'sky', split_axis=0, concat_axis=0, tiled=True)  5.32 us
  transfers between devices with their start and end apart: 4, of which 4 were waited for; matrix products, arithmetic and copies ran while one was open for 4% of the time, Pallas kernels for 5%

commit v1 on v0

--- a/solution.py
+++ b/solution.py
@@ -10,6 +10,8 @@
 DEPTHS = 2048
 STEP = 2.5
 BLK = 128
+LAG = 2
+MESH = pl.DeviceIdType.MESH
 GAIN = 0.3
 LOW = 64
 HIGH = 32
@@ -21,6 +23,7 @@
     return jnp.broadcast_to(row, (8, 128))
 
 def clean_tile(groups, chans, data_ref, picks, t_ref, r_ref, out_ref, oh, e4, ec, es):
+    per = data_ref.shape[1] // 16
     lo = picks & (LOW - 1)
     hi = picks >> 6
     for j in range(NC):
@@ -34,7 +37,7 @@
     e4[...] = jnp.dot(t_ref[...], oh[...], preferred_element_type=jnp.float32)
 
     def peak(g, acc):
-        x = data_ref[pl.ds(pl.multiple_of(g * 16, 16), 16), :].astype(jnp.float32)
+        x = data_ref[g // per, pl.ds(pl.multiple_of(g % per * 16, 16), 16), :].astype(jnp.float32)
         q, u = x[:8], x[8:]
         base = pl.multiple_of(g * 32, 32)
         out = []
@@ -75,7 +78,7 @@
 
     def model(g, _):
         rows16 = pl.ds(pl.multiple_of(g * 16, 16), 16)
-        x = data_ref[rows16, :].astype(jnp.float32)
+        x = data_ref[g // per, pl.ds(pl.multiple_of(g % per * 16, 16), 16), :].astype(jnp.float32)
         mr, mi = zero, zero
         for j in range(NC):
             c, s = ec[g * NC + j], es[g * NC + j]
@@ -87,27 +90,134 @@
 
     lax.fori_loop(0, groups, model, 0)
 
-def kernel(groups, chans, data_ref, picks_ref, t_ref, r_ref, out_ref, oh, e4, ec, es):
-    clean_tile(groups, chans, data_ref, picks_ref[...], t_ref, r_ref, out_ref, oh, e4, ec, es)
-
-def clean(data, picks, t, r, chans):
+def gather_kernel(groups, chans, send_ref, picks_ref, t_ref, r_ref, out_ref, data, res, oh, e4, ec, es, own, sa, ra, sn, rn, sf, rf, so):
+    count = lax.axis_size("freq")
+    me = lax.axis_index("freq")
+    chunks = picks_ref.shape[0]
+    half = chans
+    to_right = {"freq": lax.rem(me + 1, count)}
+    to_left = {"freq": lax.rem(me + count - 1, count)}
+    left = lax.rem(me + count - 1, count)
+    right = lax.rem(me + 1, count)
+    far = lax.rem(me + 2, count)
+
+    barrier = pltpu.get_barrier_semaphore()
+    for k in range(1, count):
+        pl.semaphore_signal(barrier, inc=1, device_id={"freq": lax.rem(me + k, count)}, device_id_type=MESH)
+    pl.semaphore_wait(barrier, count - 1)
+
+    def part(c, k):
+        peer = lax.rem(me + k, count)
+        return pltpu.make_async_remote_copy(
+            src_ref=send_ref.at[peer, c], dst_ref=data.at[c, me],
+            send_sem=sa.at[c, k], recv_sem=ra.at[c, k], device_id={"freq": peer}, device_id_type=MESH)
+
+    def arrived(c, k):
+        source = lax.rem(me + count - k, count)
+        return pltpu.make_async_remote_copy(
+            src_ref=send_ref.at[source, c], dst_ref=data.at[c, source],
+            send_sem=sa.at[c, k], recv_sem=ra.at[c, k], device_id={"freq": source}, device_id_type=MESH)
+
+    def kept(c):
+        return pltpu.make_async_copy(send_ref.at[me, c], data.at[c, me], own.at[c])
+
+    def start_parts(c, _):
+        kept(c).start()
+        for k in (1, 3, 2):
+            part(c, k).start()
+        return 0
+
+    lax.fori_loop(0, chunks, start_parts, 0)
+
+    def to_neighbour(c, way, source):
+        return pltpu.make_async_remote_copy(
+            src_ref=res.at[source, c], dst_ref=res.at[source, c],
+            send_sem=sn.at[c, way], recv_sem=rn.at[c, way],
+            device_id=to_right if way == 0 else to_left, device_id_type=MESH)
+
+    def onward(c, way, source):
+        rows = pl.ds(way * half, half)
+        return pltpu.make_async_remote_copy(
+            src_ref=res.at[source, c, rows], dst_ref=res.at[source, c, rows],
+            send_sem=sf.at[c, way], recv_sem=rf.at[c, way],
+            device_id=to_right if way == 0 else to_left, device_id_type=MESH)
+
+    def keep(c, source):
+        return pltpu.make_async_copy(res.at[source, c], out_ref.at[source, c], so.at[c, source])
+
+    def relay(c):
+        to_neighbour(c, 0, left).wait_recv()
+        onward(c, 0, left).start()
+        keep(c, left).start()
+        to_neighbour(c, 1, right).wait_recv()
+        onward(c, 1, right).start()
+        keep(c, right).start()
+
+    def step(c, _):
+        kept(c).wait()
+        for k in (1, 3, 2):
+            arrived(c, k).wait_recv()
+        clean_tile(groups, chans, data.at[c], picks_ref[c], t_ref, r_ref, res.at[me, c], oh, e4, ec, es)
+        to_neighbour(c, 0, me).start()
+        to_neighbour(c, 1, me).start()
+        keep(c, me).start()
+
+        @pl.when(c >= LAG)
+        def _():
+            relay(c - LAG)
+        return 0
+
+    lax.fori_loop(0, chunks, step, 0)
+    for c in range(chunks - LAG, chunks):
+        relay(c)
+
+    def finish(c, _):
+        onward(c, 0, far).wait_recv()
+        onward(c, 1, far).wait_recv()
+        keep(c, far).start()
+        for k in (1, 3, 2):
+            part(c, k).wait_send()
+        to_neighbour(c, 0, me).wait_send()
+        to_neighbour(c, 1, me).wait_send()
+        onward(c, 0, left).wait_send()
+        onward(c, 1, right).wait_send()
+        return 0
+
+    lax.fori_loop(0, chunks, finish, 0)
+
+    def written(c, _):
+        for source in (me, left, right, far):
+            keep(c, source).wait()
+        return 0
+
+    lax.fori_loop(0, chunks, written, 0)
+
+
+def clean_gather(send, picks, t, r, chans):
     groups = chans // 8
-    pixels = data.shape[1]
+    count, chunks, local, width = send.shape
+    dma = pltpu.SemaphoreType.DMA
+    vmem = pl.BlockSpec(memory_space=pltpu.VMEM)
     return pl.pallas_call(
-        functools.partial(kernel, groups, chans),
-        grid=(pixels // 128,),
-        in_specs=[
-            pl.BlockSpec((2 * chans, 128), lambda i: (0, i)),
-            pl.BlockSpec((NC, 128), lambda i: (0, i)),
-            pl.BlockSpec((4 * chans, 2 * (LOW + HIGH)), lambda i: (0, 0)),
-            pl.BlockSpec((2, 16, 128), lambda i: (0, 0, 0)),
+        functools.partial(gather_kernel, groups, chans),
+        in_specs=[vmem] * 4,
+        out_specs=pl.BlockSpec(memory_space=pl.ANY),
+        out_shape=jax.ShapeDtypeStruct((count, chunks, 2 * chans, width), jnp.bfloat16),
+        scratch_shapes=[
+            pltpu.VMEM((chunks, count, local, width), jnp.bfloat16),
+            pltpu.VMEM((count, chunks, 2 * chans, width), jnp.bfloat16),
+            pltpu.VMEM((2 * (LOW + HIGH), NC * width), jnp.bfloat16),
+            pltpu.VMEM((4 * chans, NC * width), jnp.float32),
+            pltpu.VMEM((groups * NC, 8, width), jnp.float32),
+            pltpu.VMEM((groups * NC, 8, width), jnp.float32),
+            dma((chunks,)), dma((chunks, count)), dma((chunks, count)),
+            dma((chunks, 2)), dma((chunks, 2)), dma((chunks, 2)), dma((chunks, 2)), dma((chunks, count)),
         ],
-        out_specs=pl.BlockSpec((2 * chans, 128), lambda i: (0, i)),
-        out_shape=jax.ShapeDtypeStruct((2 * chans, pixels), jnp.bfloat16),
-        scratch_shapes=[pltpu.VMEM((2 * (LOW + HIGH), 1024), jnp.bfloat16), pltpu.VMEM((4 * chans, 1024), jnp.float32)] + [pltpu.VMEM((groups * NC, 8, 128), jnp.float32)] * 2,
-        compiler_params=pltpu.CompilerParams(vmem_limit_bytes=40 << 20),
-        name="clean",
-    )(data, picks, t, r)
+        compiler_params=pltpu.CompilerParams(collective_id=0, has_side_effects=True, vmem_limit_bytes=48 << 20),
+        cost_estimate=pl.CostEstimate(flops=3 << 32, bytes_accessed=16 << 20, transcendentals=0),
+        name="clean_gather",
+    )(send, picks, t, r)
+
 
 def split(x):
     top = lax.reduce_precision(x, 8, 7)
@@ -151,10 +261,11 @@
 
 
 def fdf_kernel(k_ref, res_ref, out_ref, mixed):
-    rows, depths, width = res_ref.shape[0], k_ref.shape[0], res_ref.shape[2]
+    rows, depths, width = res_ref.shape[0], k_ref.shape[0], res_ref.shape[1] * 128
     for row in range(rows):
+        block = jnp.concatenate([res_ref[row, c] for c in range(width // 128)], axis=1)
         for first in range(0, depths, 256):
-            part = jnp.dot(k_ref[first:first + 256, :], res_ref[row], preferred_element_type=jnp.float32)
+            part = jnp.dot(k_ref[first:first + 256, :], block, preferred_element_type=jnp.float32)
             for c in range(width // 128):
                 mixed[c, pl.ds(first * rows + row, 256, rows), :] = part[:, c * 128:(c + 1) * 128]
     for c in range(width // 128):
@@ -163,7 +274,8 @@
 
 
 def fdf(kt, res):
-    rows, total, columns = res.shape
+    rows, chunks, total, _ = res.shape
+    columns = chunks * 128
     depths = kt.shape[0]
     width = 256
     return pl.pallas_call(
@@ -171,7 +283,7 @@
         grid=(columns // width,),
         in_specs=[
             pl.BlockSpec((depths, total), lambda i: (0, 0)),
-            pl.BlockSpec((rows, total, width), lambda i: (0, 0, i)),
+            pl.BlockSpec((rows, width // 128, total, 128), lambda i: (0, i, 0, 0)),
         ],
         out_specs=pl.BlockSpec((2, depths // 2, rows, width), lambda i: (0, 0, 0, i)),
         out_shape=jax.ShapeDtypeStruct((2, depths // 2, rows, columns), jnp.bfloat16),
@@ -199,18 +311,17 @@
     w_ref, out_ref = refs[-2], refs[-1]
     owner = pl.program_id(0)
     for rank in range(capacity):
-        value = lax.dot_general(refs[rank][0], w_ref[0], (((0,), (0,)), ((), ())), preferred_element_type=jnp.float32)
+        value = lax.dot_general(refs[rank][0, 0], w_ref[0], (((0,), (0,)), ((), ())), preferred_element_type=jnp.float32)
         out_ref[0, rank] = jnp.where(filled[owner, rank] > 0, value, 0.0).astype(jnp.bfloat16)
 
 
 def fits(chosen, filled, res, w):
     count, capacity = chosen.shape
-    rows, total, columns = res.shape
-    per_row = columns // BLK
+    _, per_row, total, _ = res.shape
     terms = w.shape[2]
 
     def pick(rank):
-        return pl.BlockSpec((1, total, BLK), lambda o, c, f: (c[o, rank] // per_row, 0, c[o, rank] % per_row))
+        return pl.BlockSpec((1, 1, total, BLK), lambda o, c, f: (c[o, rank] // per_row, c[o, rank] % per_row, 0, 0))
 
     return pl.pallas_call(
         fit_kernel,
@@ -240,11 +351,11 @@
     weights = grouped(fit_matrix[0].reshape(2, chans, -1), chans).reshape(2 * chans, -1)
     weights = lax.all_gather(weights, "sky", axis=0)
     off, t = tables(lam2)
-    outgoing = jnp.moveaxis(grouped(stokes, local), 3, 0).reshape(rows, 2 * local, columns)
-    data = lax.all_to_all(outgoing, "freq", split_axis=0, concat_axis=0, tiled=True)
+    pieces = stokes.reshape(2, local // 8, 8, rows, columns // BLK, BLK)
+    send = jnp.transpose(pieces, (3, 4, 1, 0, 2, 5)).reshape(rows, columns // BLK, 2 * local, BLK)
     picks = lax.dynamic_index_in_dim(peaks, freq, 1, keepdims=False)
-    res = clean(data.reshape(2 * chans, columns), picks, t, spread(off), chans)
-    res = lax.all_gather(res, "freq", axis=0)
+    picks = jnp.swapaxes(picks.reshape(-1, columns // BLK, BLK), 0, 1)
+    res = clean_gather(send, picks, t, spread(off), chans)
     depths = DEPTHS // freq_count
     kt = synthesis(off, freq * depths, depths)
     chosen, filled = slots_of(island_owner[:, 0], sky_count, capacity)

time: 223 us -> 145 us (0.65)
  waiting for transfers between devices: 126 us -> 11.8 us
  Pallas kernels: 50.6 us -> 85.4 us
  other arithmetic: 10.9 us -> 13.7 us
    all_gather x1 -> x0, waiting for transfers between devices: 53 us -> none  [shards(): res = lax.all_gather(res, 'freq', axis=0)]
    all_gather x1, waiting for transfers between devices: 50.6 us -> 0.02 us  [shards(): weights = lax.all_gather(weights, 'sky', axis=0)]
    pallas_call x1, Pallas kernels: 21.8 us -> 57.9 us  [clean_gather(): pl.pallas_call(functools.partial(gather_kernel, groups, chans), in_specs=...]
    all_to_all x1 -> x0, waiting for transfers between devices: 11.3 us -> none  [shards(): lax.all_to_all(outgoing, 'freq', split_axis=0, concat_axis=0, tiled=True)]
    all_to_all x1 -> x0, starting transfers between devices: 5.14 us -> none  [shards(): lax.all_to_all(outgoing, 'freq', split_axis=0, concat_axis=0, tiled=True)]
    all_to_all x1, starting transfers between devices: 5.32 us -> 9.09 us  [shards(): got = lax.all_to_all(sent, 'sky', split_axis=0, concat_axis=0, tiled=True)]
    reshape x0 -> x3, local copies, waits for them, and re-layouts: none -> 2.92 us  [the longest x2 2.92 us: shards(): pieces = stokes.reshape(2, local // 8, 8, rows, columns // BLK, BLK)]
    another operation x1 -> x0, local copies, waits for them, and re-layouts: 2.67 us -> none  [shards(): jnp.moveaxis(grouped(stokes, local), 3, 0).reshape(rows, 2 * local, columns)]
  transfers between devices with their start and end apart: 4 -> 2, of which waited for: 4 -> 1; matrix products, arithmetic and copies ran while one was open for 4% -> 10% of each run, Pallas kernels for 5% -> 48%
where the time goes in v1:
time: 145 us
  Pallas kernels  85.4 us (59%)
  between operations  14.9 us (10%)
  other arithmetic  13.7 us (9%)
  waiting for transfers between devices  11.8 us (8%)
  local copies, waits for them, and re-layouts  9.67 us (7%)
  starting transfers between devices  9.12 us (6%)
    pallas_call x1, Pallas kernels, clean_gather(): pl.pallas_call(functools.partial(gather_kernel, groups, chans), in_specs=...  57.9 us
    pallas_call x1, Pallas kernels, fits(): pl.pallas_call(fit_kernel, grid_spec=pltpu.PrefetchScalarGridSpec(num_sca...  16.2 us
    all_to_all x1, waiting for transfers between devices, shards(): got = lax.all_to_all(sent, 'sky', split_axis=0, concat_axis=0, tiled=True)  11.7 us
    pallas_call x1, Pallas kernels, fdf(): pl.pallas_call(fdf_kernel, grid=(columns // width,), in_specs=[pl.BlockSp...  11.4 us
    all_to_all x1, starting transfers between devices, shards(): got = lax.all_to_all(sent, 'sky', split_axis=0, concat_axis=0, tiled=True)  9.09 us
    select_n x1, other arithmetic, synthesis(): real = jnp.where(is_u, sine, cosine)  4.75 us
    unnamed x8, local copies, waits for them, and re-layouts  4.68 us
    reshape x2, local copies, waits for them, and re-layouts, shards(): pieces = stokes.reshape(2, local // 8, 8, rows, columns // BLK, BLK)  2.92 us
  transfers between devices with their start and end apart: 2, of which 1 were waited for; matrix products, arithmetic and copies ran while one was open for 10% of the time, Pallas kernels for 48%

profile of v1, /device:TPU:1, one launch (start us, length us, event | category | flops | bytes accessed | tf_op | source)
XLA Modules:
  0.0 144.9 jit_solution(5428084995304399176)
XLA Ops:
  7.2 0.0 copy-start
  7.2 0.0 all-gather.2.cloned.1.call-start
  7.2 1.6 %copy.17 = bf16[2,36,8,128]{3,2,0,1:T(8,128)(2,1)} copy(bf16[2,36,8,128]{3,2,1,0:T(8,128)(2,1)} %bitcast.29) | data formatting | bytes 294912 | tf_op jit(solution)/shard_map/reshape;reshape;squeeze | solution.py:342
  8.9 0.0 all-gather.2.cloned.1.call-update
  8.9 0.9 convert_reduce_fusion
  9.9 0.7 iota_compare_fusion.1
  10.5 0.2 fusion.12
  10.7 0.1 copy.19.filled
  10.8 0.1 copy.18.chosen
  10.8 1.3 reduce_sum.36
  12.8 0.7 subtract_multiply_fusion
  13.5 0.1 mul.173
  13.6 0.0 copy-done
  13.6 2.5 %reshape.256 = bf16[2,9,8,4,8,128]{5,4,3,2,1,0:T(8,128)(2,1)S(1)} reshape(bf16[2,72,4,1024]{3,2,1,0:T(4,128)(2,1)} %param.5) | data formatting | bytes 2359296 | tf_op jit(solution)/shard_map/reshape | solution.py:354
  16.1 0.5 copy.15
  16.6 0.2 multiply_cosine_fusion.4
  16.8 0.1 maximum_bitcast_fusion.2
  16.9 0.6 multiply_cosine_fusion.1
  17.5 0.3 convolution_multiply_fusion.r_ref
  17.8 0.6 multiply_cosine_fusion.2
  18.4 0.1 reduce-precision_convert_fusion
  18.4 0.6 multiply_cosine_fusion.3
  19.0 0.1 reduce-precision_convert_fusion.1
  19.1 0.3 maximum_maximum_fusion
  19.3 57.9 %clean_gather.1.res_ref.refs_0_.refs_1_ = bf16[4,8,576,128]{3,2,1,0:T(8,128)(2,1)} custom-call(bf16[4,8,144,128]{3,2,1,0:T(8,128)(2,1)S(1)} %bitcast.25, s32[8,8,128]{2,1,0:T(8,128)S(1)} %bitcast.27, bf16[1152,192]{1,0:T(8,128)(2,1)S(1)} %bitcast.26, f32[2,16,128]{2,1,0:T(8,128)S(1)} %convolution_multiply_fusion.r_ref), custom_call_target="tpu_custom_call" | custom-call | flops 12884901888 | bytes 16777216 | tf_op jit(solution)/shard_map/clean_gather/pallas_call | solution.py:201
  77.2 0.0 all-gather.2.cloned.1.call-done.refs_2_
  77.2 0.0 copy-start.1
  77.2 2.3 %copy-done.1 = bf16[4,8,576,128]{3,2,1,0:T(8,128)(2,1)S(1)} copy-done((bf16[4,8,576,128]{3,2,1,0:T(8,128)(2,1)S(1)}, bf16[4,8,576,128]{3,2,1,0:T(8,128)(2,1)}, u32[]{:S(2)}) %copy-start.1) | copy-done | bytes 4718616
  79.6 0.0 copy-start.3
  79.6 2.3 %copy-done.3 = bf16[32,576,128]{2,1,0:T(8,128)(2,1)S(1)} copy-done((bf16[32,576,128]{2,1,0:T(8,128)(2,1)S(1)}, bf16[32,576,128]{2,1,0:T(8,128)(2,1)}, u32[]{:S(2)}) %copy-start.3) | copy-done | bytes 4718616
  81.9 16.2 %fits.1 = bf16[32,2,128,128]{3,2,1,0:T(8,128)(2,1)} custom-call(s32[32,2]{1,0:T(8,128)S(1)} %copy.18.chosen, s32[32,2]{1,0:T(8,128)S(1)} %copy.19.filled, bf16[4,8,576,128]{3,2,1,0:T(8,128)(2,1)S(1)} %copy-done.1, bf16[4,8,576,128]{3,2,1,0:T(8,128)(2,1)S(1)} %copy-done.1, bf16[32,576,128]{2,1,0:T(8,128)(2,1)S(1)} %copy-done.3), custom_call_target="tpu_custom_call" | custom-call | tf_op jit(solution)/shard_map/fits/pallas_call | solution.py:326
  98.1 9.1 %all-to-all-start = ((bf16[32,2,128,128]{3,2,1,0:T(8,128)(2,1)}), bf16[32,2,128,128]{3,2,1,0:T(8,128)(2,1)S(1)}, u32[]{:S(2)}, u32[]{:S(2)}) async-start(bf16[32,2,128,128]{3,2,1,0:T(8,128)(2,1)} %fits.1), calls=%async_computation | async-start | bytes 4194304 | tf_op jit(solution)/shard_map/all_to_all | solution.py:363
  107.2 0.1 mul.174
  107.4 0.0 copy-start.2
  107.4 4.7 %fusion.2 = (f32[512,576]{1,0:T(8,128)S(1)}, f32[512,576]{1,0:T(8,128)S(1)}) fusion(f32[512]{0:T(512)S(1)} %convert_multiply_fusion, f32[576]{0:T(1024)S(1)} %mul.174, pred[576]{0:T(1024)(128)(4,1)S(1)} %fusion.17), kind=kLoop, calls=%fused_computation.6 | loop fusion | flops 1179648 | bytes 2364224 | tf_op jit(solution)/shard_map/jit(_where)/select_n | solution.py:258
  112.1 0.3 fusion.k_ref
  112.4 0.0 copy-done.2
  112.4 11.4 %fdf.1 = bf16[2,512,4,1024]{3,2,1,0:T(4,128)(2,1)} custom-call(bf16[1024,576]{1,0:T(8,128)(2,1)S(1)} %fusion.k_ref, bf16[4,8,576,128]{3,2,1,0:T(8,128)(2,1)S(1)} %copy-done.2), custom_call_target="tpu_custom_call" | custom-call | flops 4831838208 | bytes 14680064 | tf_op jit(solution)/shard_map/fdf/pallas_call | solution.py:281
  123.8 11.7 %all-to-all-done = bf16[32,2,128,128]{3,2,1,0:T(8,128)(2,1)S(1)} async-done(((bf16[32,2,128,128]{3,2,1,0:T(8,128)(2,1)}), bf16[32,2,128,128]{3,2,1,0:T(8,128)(2,1)S(1)}, u32[]{:S(2)}, u32[]{:S(2)}) %all-to-all-start) | async-done | bytes 2097184 | tf_op jit(solution)/shard_map/all_to_all | solution.py:363
  135.5 2.5 %bitcast_convert_fusion = f32[1,32,2,128,128]{4,3,2,1,0:T(8,128)} fusion(bf16[32,2,128,128]{3,2,1,0:T(8,128)(2,1)S(1)} %all-to-all-done), kind=kLoop, calls=%fused_computation.2 | loop fusion | flops 1048576 | bytes 6291456 | tf_op jit(solution)/shard_map/broadcast_in_dim | solution.py:364
  (14 shorter events, 0.1 us)
Async XLA Ops:
  7.2 6.4 %copy-start = (s32[8,4,1024]{2,1,0:T(4,128)S(1)}, s32[8,4,1024]{2,1,0:T(4,128)}, u32[]{:S(2)}) copy-start(s32[8,4,1024]{2,1,0:T(4,128)} %param.7) | copy-start | bytes 393220
  7.2 70.0 %all-gather.2.cloned.1.call-start = ((), (), s32[]{:S(2)}) async-start(), calls=%async_computation.1 | async-start | bytes 4866048 | tf_op jit(solution)/shard_map/all_gather | solution.py:352
  77.2 2.3 %copy-start.1 = (bf16[4,8,576,128]{3,2,1,0:T(8,128)(2,1)S(1)}, bf16[4,8,576,128]{3,2,1,0:T(8,128)(2,1)}, u32[]{:S(2)}) copy-start(bf16[4,8,576,128]{3,2,1,0:T(8,128)(2,1)} %clean_gather.1.res_ref.refs_0_.refs_1_) | copy-start | bytes 14155780
  79.6 2.3 %copy-start.3 = (bf16[32,576,128]{2,1,0:T(8,128)(2,1)S(1)}, bf16[32,576,128]{2,1,0:T(8,128)(2,1)}, u32[]{:S(2)}) copy-start(bf16[32,576,128]{2,1,0:T(8,128)(2,1)} %all-gather.2.cloned.1.call-done.refs_2_) | copy-start | bytes 14155780
  98.1 37.4 %all-to-all-start = ((bf16[32,2,128,128]{3,2,1,0:T(8,128)(2,1)}), bf16[32,2,128,128]{3,2,1,0:T(8,128)(2,1)S(1)}, u32[]{:S(2)}, u32[]{:S(2)}) async-start(bf16[32,2,128,128]{3,2,1,0:T(8,128)(2,1)} %fits.1), calls=%async_computation | async-start | bytes 4194304 | tf_op jit(solution)/shard_map/all_to_all | solution.py:363
  107.4 5.0 %copy-start.2 = (bf16[4,8,576,128]{3,2,1,0:T(8,128)(2,1)S(1)}, bf16[4,8,576,128]{3,2,1,0:T(8,128)(2,1)}, u32[]{:S(2)}) copy-start(bf16[4,8,576,128]{3,2,1,0:T(8,128)(2,1)} %clean_gather.1.res_ref.refs_0_.refs_1_) | copy-start | bytes 14155780
Sparse Core Ops, SparseCore 0:
  10.8 50.7 all-gather.1

commit v2 on v0

v2 whole, which is shorter than its diff:
```python
import functools
import jax
import jax.numpy as jnp
from jax import lax
from jax.sharding import PartitionSpec as P
from jax.experimental import pallas as pl
from jax.experimental.pallas import tpu as pltpu

NC = 8
DEPTHS = 2048
STEP = 2.5
BLK = 128
LAG = 2
MESH = pl.DeviceIdType.MESH
GAIN = 0.3
LOW = 64

def gather(x, idx):
    return jnp.take_along_axis(x, idx, axis=1, mode="promise_in_bounds")


def full(row):
    return jnp.broadcast_to(row, (8, 128))


def make_tables(chans, column_ref, row_ref, t, near, spread):
    mean = jnp.sum(row_ref[...], axis=1, keepdims=True) / chans
    lane = lax.broadcasted_iota(jnp.int32, (8, 128), 1)
    low = lane < LOW
    depth = jnp.where(low, lane, (lane - LOW) * LOW - DEPTHS // 2).astype(jnp.float32) * STEP
    plain = lane.astype(jnp.float32) * STEP

    def rows(g, _):
        twice = 2.0 * (column_ref[pl.ds(pl.multiple_of(g * 8, 8), 8), :] - mean)
        angle = twice * depth
        parts = []
        for mask in (low, ~low):
            for value in (jnp.cos(angle), jnp.sin(angle)):
                value = jnp.where(mask, value, 0.0)
                top = value.astype(jnp.bfloat16)
                parts.append(jnp.concatenate([top, (value - top.astype(jnp.float32)).astype(jnp.bfloat16)], axis=1))
        t[pl.ds(pl.multiple_of(g * 32, 32), 32), :] = jnp.concatenate(parts, axis=0)
        angle = twice * plain
        near[0, pl.ds(pl.multiple_of(g * 8, 8), 8), :] = jnp.cos(angle)
        near[1, pl.ds(pl.multiple_of(g * 8, 8), 8), :] = jnp.sin(angle)
        return 0

    lax.fori_loop(0, chans // 8, rows, 0)
    twice = 2.0 * (row_ref[...] - mean)
    angle = twice * (lax.broadcasted_iota(jnp.int32, (16, chans), 0).astype(jnp.float32) * (128 * STEP))
    cosine, sine = jnp.cos(angle), jnp.sin(angle)
    dot = functools.partial(jnp.dot, precision=lax.Precision.HIGHEST, preferred_element_type=jnp.float32)
    spread[0] = (dot(cosine, near[0]) - dot(sine, near[1])) / chans
    spread[1] = -(dot(sine, near[0]) + dot(cosine, near[1])) / chans


def clean_tile(chans, row, rows, data, picks, t, spread, out_ref, oh, e4, ec, es):
    groups = chans // 8
    lo = picks & (LOW - 1)
    hi = (picks >> 6) + LOW
    index = lax.broadcasted_iota(jnp.int32, (128, 128), 0)
    for j in range(NC):
        cols = slice(j * 128, (j + 1) * 128)
        hot = ((index == lo[j:j+1]) | (index == hi[j:j+1])).astype(jnp.bfloat16)
        oh[0:128, cols] = hot
        oh[128:256, cols] = hot
    e4[...] = jnp.dot(t[...], oh[...], preferred_element_type=jnp.float32)

    def planes(g):
        at = pl.ds(g * (8 * rows) + row, 8, rows)
        return data[0, at, :], data[1, at, :]

    def peak(g, acc):
        q, u = planes(g)
        base = pl.multiple_of(g * 32, 32)
        out = []
        for j in range(NC):
            cols = slice(j * 128, (j + 1) * 128)
            cl, sl = e4[pl.ds(base, 8), cols], e4[pl.ds(base + 8, 8), cols]
            ch, sh = e4[pl.ds(base + 16, 8), cols], e4[pl.ds(base + 24, 8), cols]
            c = ch * cl - sh * sl
            s = sh * cl + ch * sl
            ec[g * NC + j] = c
            es[g * NC + j] = s
            out.append((acc[j][0] + (q * c + u * s), acc[j][1] + (u * c - q * s)))
        return tuple(out)

    zero = jnp.zeros((8, 128), jnp.float32)
    acc = lax.fori_loop(0, groups, peak, tuple((zero, zero) for _ in range(NC)))
    scale = 1.0 / chans
    vr = jnp.concatenate([jnp.sum(a[0], axis=0, keepdims=True) for a in acc], axis=0) * scale
    vi = jnp.concatenate([jnp.sum(a[1], axis=0, keepdims=True) for a in acc], axis=0) * scale
    comps = []
    for i in range(NC):
        cr = full(vr[i:i+1] * GAIN)
        ci = full(vi[i:i+1] * GAIN)
        comps.append((cr, ci))
        if i == NC - 1:
            break
        d = picks - picks[i:i+1]
        a = jnp.abs(d)
        alo, ahi = a & 127, a >> 7
        rr, ri = zero, zero
        for h in range(16):
            here = ahi == h
            rr = jnp.where(here, gather(full(spread[0, h:h+1, :]), alo), rr)
            ri = jnp.where(here, gather(full(spread[1, h:h+1, :]), alo), ri)
        ri = jnp.where(d < 0, -ri, ri)
        vr = vr - (cr * rr - ci * ri)
        vi = vi - (cr * ri + ci * rr)

    def model(pair, _):
        real, imag = [], []
        for part in range(2):
            g = pair * 2 + part
            q, u = planes(g)
            mr, mi = zero, zero
            for j in range(NC):
                c, s = ec[g * NC + j], es[g * NC + j]
                cr, ci = comps[j]
                mr = mr + (cr * c - ci * s)
                mi = mi + (cr * s + ci * c)
            real.append(q - mr)
            imag.append(u - mi)
        out_ref[pl.ds(pl.multiple_of(pair * 16, 16), 16), :] = jnp.concatenate(real, axis=0).astype(jnp.bfloat16)
        out_ref[pl.ds(pl.multiple_of(chans + pair * 16, 16), 16), :] = jnp.concatenate(imag, axis=0).astype(jnp.bfloat16)
        return 0

    lax.fori_loop(0, groups // 2, model, 0)


def island_kernel(chans, stokes_ref, column_ref, row_ref, picks_ref, owner_ref, w_ref, out_ref, sent_ref,
                  raw, data, res, w, fit, t, near, spread, oh, e4, ec, es, chosen,
                  own, sa, ra, sn, rn, sf, rf, so, ow, sw, rw, sc, rc):
    count = lax.axis_size("freq")
    me = lax.axis_index("freq")
    sky = lax.axis_index("sky")
    x, z, core = sky // 8, sky // 2 % 4, sky % 2
    chunks, rows = picks_ref.shape[0], stokes_ref.shape[2]
    tiles = chunks // rows
    local = stokes_ref.shape[1]
    half = chans
    left, right, far = [lax.rem(me + k, count) for k in (count - 1, 1, 2)]

    def at_x(k):
        return {"sky": lax.rem(x + k, 4) * 8 + z * 2 + core}

    def at_z(k):
        return {"sky": x * 8 + lax.rem(z + k, 4) * 2 + core}

    other = {"sky": sky + 1 - 2 * core}

    barrier = pltpu.get_barrier_semaphore()
    for k in range(1, 4):
        pl.semaphore_signal(barrier, inc=1, device_id={"freq": lax.rem(me + k, count)}, device_id_type=MESH)
        pl.semaphore_signal(barrier, inc=1, device_id=at_x(k), device_id_type=MESH)
        pl.semaphore_signal(barrier, inc=1, device_id=at_z(k), device_id_type=MESH)
    pl.semaphore_signal(barrier, inc=1, device_id=other, device_id_type=MESH)
    pl.semaphore_wait(barrier, 10)

    def columns(owner, tile):
        return pl.ds(pl.multiple_of((owner * tiles + tile) * 128, 128), 128)

    def part(tile, k):
        peer = lax.rem(me + k, count)
        return pltpu.make_async_remote_copy(
            src_ref=stokes_ref.at[:, :, :, columns(peer, tile)], dst_ref=raw.at[tile, me],
            send_sem=sa.at[tile, k], recv_sem=ra.at[tile, k], device_id={"freq": peer}, device_id_type=MESH)

    def arrived(tile, k):
        source = lax.rem(me + count - k, count)
        return pltpu.make_async_remote_copy(
            src_ref=stokes_ref.at[:, :, :, columns(me, tile)], dst_ref=raw.at[tile, source],
            send_sem=sa.at[tile, k], recv_sem=ra.at[tile, k], device_id={"freq": source}, device_id_type=MESH)

    def kept(tile):
        return pltpu.make_async_copy(stokes_ref.at[:, :, :, columns(me, tile)], raw.at[tile, me], own.at[tile])

    for tile in range(tiles):
        kept(tile).start()
        for k in (1, 3, 2):
            part(tile, k).start()
    pltpu.make_async_copy(w_ref.at[0], w.at[x, z, core], ow).start()
    pltpu.make_async_copy(w_ref.at[0], w.at[x, z, core], ow).wait()

    def w_first(h, k, source=None):
        along_x = h == 0
        lines = pl.ds(h * half, half)
        piece = w.at[x, z, core, lines]
        if source is not None:
            piece = w.at[lax.rem(x + 4 - k, 4), z, core, lines] if along_x else w.at[x, lax.rem(z + 4 - k, 4), core, lines]
        return pltpu.make_async_remote_copy(
            src_ref=piece, dst_ref=piece, send_sem=sw.at[0, h, k], recv_sem=rw.at[0, h, k],
            device_id=at_x(k) if along_x else at_z(k), device_id_type=MESH)

    def w_second(h, k, source=None):
        along_x = h == 1
        lines = pl.ds(h * half, half)
        back = k if source is not None else 4
        if along_x:
            piece = w.at[lax.rem(x + 4 - back + (4 if back == 4 else 0), 4), :, core, lines]
        else:
            piece = w.at[:, lax.rem(z + 4 - back + (4 if back == 4 else 0), 4), core, lines]
        return pltpu.make_async_remote_copy(
            src_ref=piece, dst_ref=piece, send_sem=sw.at[1, h, k], recv_sem=rw.at[1, h, k],
            device_id=at_x(k) if along_x else at_z(k), device_id_type=MESH)

    def w_third(which):
        piece = w.at[:, :, which]
        return pltpu.make_async_remote_copy(
            src_ref=piece, dst_ref=piece, send_sem=sc, recv_sem=rc, device_id=other, device_id_type=MESH)

    for h in range(2):
        for k in range(1, 4):
            w_first(h, k).start()

    def slot(o, _):
        first, second = jnp.int32(-1), jnp.int32(-1)
        for b in reversed(range(owner_ref.shape[0])):
            hit = owner_ref[b] == o
            second = jnp.where(hit, first, second)
            first = jnp.where(hit, b, first)
        chosen[o * 2] = first
        chosen[o * 2 + 1] = second
        return 0

    lax.fori_loop(0, sent_ref.shape[0], slot, 0)
    make_tables(chans, column_ref, row_ref, t, near, spread)

    def to_neighbour(c, way, source):
        return pltpu.make_async_remote_copy(
            src_ref=res.at[source, c], dst_ref=res.at[source, c],
            send_sem=sn.at[c, way], recv_sem=rn.at[c, way],
            device_id={"freq": right if way == 0 else left}, device_id_type=MESH)

    def onward(c, way, source):
        piece = res.at[source, c, pl.ds(way * half, half)]
        return pltpu.make_async_remote_copy(
            src_ref=piece, dst_ref=piece, send_sem=sf.at[c, way], recv_sem=rf.at[c, way],
            device_id={"freq": right if way == 0 else left}, device_id_type=MESH)

    def keep(c, source):
        return pltpu.make_async_copy(res.at[source, c], out_ref.at[source, c], so.at[c, source])

    def relay(c):
        to_neighbour(c, 0, left).wait_recv()
        onward(c, 0, left).start()
        keep(c, left).start()
        to_neighbour(c, 1, right).wait_recv()
        onward(c, 1, right).start()
        keep(c, right).start()

    def step(c, _):
        tile, row = c // rows, c % rows

        @pl.when(row == 0)
        def _():
            kept(tile).wait()
            for k in (1, 3, 2):
                arrived(tile, k).wait_recv()
            for source in range(count):
                for plane in range(2):
                    block = raw[tile, source, plane].reshape(local * rows, 128)
                    data[plane, source * local * rows:(source + 1) * local * rows, :] = block.astype(jnp.float32)

        clean_tile(chans, row, rows, data, picks_ref[c], t, spread, res.at[me, c], oh, e4, ec, es)
        to_neighbour(c, 0, me).start()
        to_neighbour(c, 1, me).start()
        keep(c, me).start()

        @pl.when(c >= LAG)
        def _():
            relay(c - LAG)

        @pl.when(c == 1)
        def _():
            for h in range(2):
                for k in range(1, 4):
                    w_first(h, k, True).wait_recv()
            for h in range(2):
                for k in range(1, 4):
                    w_second(h, k).start()

        @pl.when(c == 5)
        def _():
            for h in range(2):
                for k in range(1, 4):
                    w_second(h, k, True).wait_recv()
            w_third(core).start()

        return 0

    lax.fori_loop(0, chunks, step, 0)
    w_third(1 - core).wait_recv()

    def fit_block(source, c):
        b = c % rows * (count * tiles) + source * tiles + c // rows
        o = owner_ref[b]
        value = lax.dot_general(res[source, c], w[o >> 3, (o >> 1) & 3, o & 1], (((0,), (0,)), ((), ())),
                                preferred_element_type=jnp.float32)
        fit[b] = value.astype(jnp.bfloat16)

    def fit_some(sources, first, last):
        def some(c, _):
            for source in sources:
                fit_block(source, c)
            return 0
        lax.fori_loop(first, last, some, 0)

    fit_some((me,), 0, chunks)
    relay(chunks - 2)
    fit_some((left, right), 0, chunks // 2)
    relay(chunks - 1)
    fit_some((left, right), chunks // 2, chunks)

    def last(c, _):
        onward(c, 0, far).wait_recv()
        onward(c, 1, far).wait_recv()
        keep(c, far).start()
        fit_block(far, c)
        return 0

    lax.fori_loop(0, chunks, last, 0)

    def fill(o, _):
        for rank in range(2):
            b = chosen[o * 2 + rank]
            value = fit[jnp.maximum(b, 0)]
            sent_ref[o, rank] = jnp.where(b >= 0, value, jnp.zeros_like(value))
        return 0

    lax.fori_loop(0, sent_ref.shape[0], fill, 0)

    for tile in range(tiles):
        for k in (1, 3, 2):
            part(tile, k).wait_send()
    for h in range(2):
        for k in range(1, 4):
            w_first(h, k).wait_send()
            w_second(h, k).wait_send()
    w_third(core).wait_send()

    def finish(c, _):
        to_neighbour(c, 0, me).wait_send()
        to_neighbour(c, 1, me).wait_send()
        onward(c, 0, left).wait_send()
        onward(c, 1, right).wait_send()
        for source in (me, left, right, far):
            keep(c, source).wait()
        return 0

    lax.fori_loop(0, chunks, finish, 0)


def islands(stokes, lam2, picks, owners, weights, freq_count, sky_count):
    chans, local, rows = lam2.shape[0], stokes.shape[1], stokes.shape[2]
    groups = chans // 8
    chunks = picks.shape[0]
    terms = weights.shape[2]
    dma = pltpu.SemaphoreType.DMA
    vmem = pl.BlockSpec(memory_space=pltpu.VMEM)
    smem = pl.BlockSpec(memory_space=pltpu.SMEM)
    hbm = pl.BlockSpec(memory_space=pl.ANY)
    f32, bf16 = jnp.float32, jnp.bfloat16
    return pl.pallas_call(
        functools.partial(island_kernel, chans),
        in_specs=[hbm, vmem, vmem, vmem, smem, hbm],
        out_specs=[hbm, vmem],
        out_shape=[
            jax.ShapeDtypeStruct((freq_count, chunks, 2 * chans, 128), bf16),
            jax.ShapeDtypeStruct((sky_count, 2, BLK, terms), bf16),
        ],
        scratch_shapes=[
            pltpu.VMEM((chunks // rows, freq_count, 2, local, rows, 128), bf16),
            pltpu.VMEM((2, chans * rows, 128), f32),
            pltpu.VMEM((freq_count, chunks, 2 * chans, 128), bf16),
            pltpu.VMEM((4, 4, 2, 2 * chans, terms), bf16),
            pltpu.VMEM((freq_count * chunks, BLK, terms), bf16),
            pltpu.VMEM((4 * chans, 256), bf16),
            pltpu.VMEM((2, chans, 128), f32),
            pltpu.VMEM((2, 16, 128), f32),
            pltpu.VMEM((256, NC * 128), bf16),
            pltpu.VMEM((4 * chans, NC * 128), f32),
            pltpu.VMEM((groups * NC, 8, 128), f32),
            pltpu.VMEM((groups * NC, 8, 128), f32),
            pltpu.SMEM((sky_count * 2,), jnp.int32),
            dma((chunks // rows,)), dma((chunks // rows, 4)), dma((chunks // rows, 4)),
            dma((chunks, 2)), dma((chunks, 2)), dma((chunks, 2)), dma((chunks, 2)), dma((chunks, 4)),
            dma, dma((2, 2, 4)), dma((2, 2, 4)), dma, dma,
        ],
        compiler_params=pltpu.CompilerParams(collective_id=0, has_side_effects=True, vmem_limit_bytes=50 << 20),
        cost_estimate=pl.CostEstimate(flops=3 << 32, bytes_accessed=16 << 20, transcendentals=0),
        name="islands",
    )(stokes, lam2.reshape(chans, 1), lam2.reshape(1, chans), picks, owners, weights)


def synthesis(lam2, first, count):
    chans = lam2.shape[0]
    off = lam2 - jnp.mean(lam2)
    depth = (jnp.arange(count) + first - DEPTHS // 2).astype(jnp.float32) * STEP
    angle = (2.0 * off) * depth[:, None]
    cosine, sine = jnp.cos(angle), jnp.sin(angle)
    real = jnp.concatenate([cosine, sine], axis=1)
    imag = jnp.concatenate([-sine, cosine], axis=1)
    return (jnp.concatenate([real, imag], axis=0) / chans).astype(jnp.bfloat16)


def fdf_kernel(k_ref, res_ref, out_ref, mixed):
    rows, depths = res_ref.shape[2], k_ref.shape[0]
    for pair in range(0, rows, 2):
        block = jnp.concatenate([res_ref[0, 0, pair], res_ref[0, 0, pair + 1]], axis=1)
        for first in range(0, depths, 256):
            part = jnp.dot(k_ref[first:first + 256, :], block, preferred_element_type=jnp.float32)
            for row in range(2):
                mixed[pl.ds(first * rows + pair + row, 256, rows), :] = part[:, row * 128:(row + 1) * 128]
    out_ref[...] = mixed[...].astype(jnp.bfloat16).reshape(out_ref.shape)


def fdf(kt, res, rows):
    count, chunks, total, _ = res.shape
    tiles = chunks // rows
    depths = kt.shape[0]
    columns = count * tiles * 128
    return pl.pallas_call(
        fdf_kernel,
        grid=(count * tiles,),
        in_specs=[
            pl.BlockSpec((depths, total), lambda i: (0, 0)),
            pl.BlockSpec((1, 1, rows, total, 128), lambda i: (i // tiles, i % tiles, 0, 0, 0)),
        ],
        out_specs=pl.BlockSpec((2, depths // 2, rows, 128), lambda i: (0, 0, 0, i)),
        out_shape=jax.ShapeDtypeStruct((2, depths // 2, rows, columns), jnp.bfloat16),
        scratch_shapes=[pltpu.VMEM((depths * rows, 128), jnp.float32)],
        compiler_params=pltpu.CompilerParams(vmem_limit_bytes=48 << 20),
        cost_estimate=pl.CostEstimate(flops=2 * depths * total * rows * columns, bytes_accessed=14 << 20, transcendentals=0),
        name="fdf",
    )(kt, res.reshape(count, tiles, rows, total, 128))


def shards(stokes, lam2, peaks, island_owner, fit_matrix):
    freq = lax.axis_index("freq")
    freq_count, sky_count = lax.axis_size("freq"), lax.axis_size("sky")
    rows, columns = stokes.shape[2], stokes.shape[3]
    mine = columns // freq_count
    picks = lax.dynamic_slice_in_dim(peaks, freq * mine, mine, 2)
    picks = jnp.transpose(picks.reshape(NC, rows, mine // 128, 128), (2, 1, 0, 3)).reshape(-1, NC, 128)
    res, sent = islands(stokes, lam2, picks, island_owner[:, 0], fit_matrix, freq_count, sky_count)
    depths = DEPTHS // freq_count
    kt = synthesis(lam2, freq * depths, depths)
    got = lax.all_to_all(sent, "sky", split_axis=0, concat_axis=0, tiled=True)
    return fdf(kt, res, rows), got.astype(jnp.float32)[None]


def solution(mesh):
    in_specs = (
        P(None, "freq", "sky", None),
        P(),
        P(None, "sky", None),
        P("sky", None),
        P("sky", None, "freq"),
    )
    out_specs = (P(None, "freq", "sky", None), P("sky", None, None, None, "freq"))
    return jax.shard_map(shards, mesh=mesh, in_specs=in_specs, out_specs=out_specs, check_vma=False)
```

time: 223 us -> 106 us (0.48)
  waiting for transfers between devices: 126 us -> 12.9 us
  Pallas kernels: 50.6 us -> 73.5 us
  between operations: 14.9 us -> 1.4 us
  other arithmetic: 10.9 us -> 6.51 us
  local copies, waits for them, and re-layouts: 8.5 us -> 4.39 us
  starting transfers between devices: 10.5 us -> 6.85 us
    all_gather x2 -> x0, waiting for transfers between devices: 104 us -> none  [the longest x1 53 us: shards(): res = lax.all_gather(res, 'freq', axis=0)]
    pallas_call x3 -> x2, Pallas kernels: 50.6 us -> 73.5 us  [the longest x1 62.8 us: islands(): pl.pallas_call(functools.partial(island_kernel, chans), in_specs=[hbm, vm...]
    all_to_all x1 -> x0, waiting for transfers between devices: 11.3 us -> none  [shards(): lax.all_to_all(outgoing, 'freq', split_axis=0, concat_axis=0, tiled=True)]
    all_to_all x1 -> x0, starting transfers between devices: 5.14 us -> none  [shards(): lax.all_to_all(outgoing, 'freq', split_axis=0, concat_axis=0, tiled=True)]
    select_n x1 -> x0, other arithmetic: 4.75 us -> none  [synthesis(): real = jnp.where(is_u, sine, cosine)]
    another operation x2 -> x0, local copies, waits for them, and re-layouts: 3.36 us -> none  [the longest x1 2.67 us: shards(): jnp.moveaxis(grouped(stokes, local), 3, 0).reshape(rows, 2 * local, columns)]
    sin x0 -> x1, other arithmetic: none -> 2.83 us  [synthesis(): cosine, sine = (jnp.cos(angle), jnp.sin(angle))]
    unnamed x15 -> x12, local copies, waits for them, and re-layouts: 4.71 us -> 2.85 us
  transfers between devices with their start and end apart: 4 -> 1, of which waited for: 4 -> 1; matrix products, arithmetic and copies ran while one was open for 4% -> 4% of each run, Pallas kernels for 5% -> 10%
where the time goes in v2:
time: 106 us
  Pallas kernels  73.5 us (69%)
  waiting for transfers between devices  12.9 us (12%)
  starting transfers between devices  6.85 us (6%)
  other arithmetic  6.51 us (6%)
  local copies, waits for them, and re-layouts  4.39 us (4%)
  between operations  1.4 us (1%)
    pallas_call x1, Pallas kernels, islands(): pl.pallas_call(functools.partial(island_kernel, chans), in_specs=[hbm, vm...  62.8 us
    all_to_all x1, waiting for transfers between devices, shards(): got = lax.all_to_all(sent, 'sky', split_axis=0, concat_axis=0, tiled=True)  12.9 us
    pallas_call x1, Pallas kernels, fdf(): pl.pallas_call(fdf_kernel, grid=(count * tiles,), in_specs=[pl.BlockSpec(...  10.7 us
    all_to_all x1, starting transfers between devices, shards(): got = lax.all_to_all(sent, 'sky', split_axis=0, concat_axis=0, tiled=True)  6.85 us
    unnamed x12, local copies, waits for them, and re-layouts  2.85 us
    sin x1, other arithmetic, synthesis(): cosine, sine = (jnp.cos(angle), jnp.sin(angle))  2.83 us
    broadcast_in_dim x1, other arithmetic, shards(): return (fdf(kt, res, rows), got.astype(jnp.float32)[None])  2.54 us
  transfers between devices with their start and end apart: 1, of which 1 were waited for; matrix products, arithmetic and copies ran while one was open for 4% of the time, Pallas kernels for 10%

profile of v2, /device:TPU:1, one launch (start us, length us, event | category | flops | bytes accessed | tf_op | source)
XLA Modules:
  0.0 105.6 jit_solution(5172437176856542346)
XLA Ops:
  0.6 0.0 copy-start
  0.6 0.8 reshape.33.column_ref
  1.5 0.7 reshape.28.row_ref
  2.2 0.0 copy-done
  2.2 0.0 copy-start.1
  2.2 1.3 %copy-done.1 = bf16[2,72,4,1024]{3,2,1,0:T(4,128)(2,1)S(1)} copy-done((bf16[2,72,4,1024]{3,2,1,0:T(4,128)(2,1)S(1)}, bf16[2,72,4,1024]{3,2,1,0:T(4,128)(2,1)}, u32[]{:S(2)}) %copy-start.1) | copy-done | bytes 1179672
  3.5 0.0 copy-start.2
  3.5 0.9 copy-done.2
  4.4 0.0 copy-start.3
  4.4 0.7 copy-done.3
  5.1 62.8 %islands.1 = (bf16[4,8,576,128]{3,2,1,0:T(8,128)(2,1)}, bf16[32,2,128,128]{3,2,1,0:T(8,128)(2,1)}) custom-call(bf16[2,72,4,1024]{3,2,1,0:T(4,128)(2,1)S(1)} %copy-done.1, f32[288,1]{1,0:T(8,128)S(1)} %reshape.33.column_ref, f32[1,288]{1,0:T(1,128)S(1)} %reshape.28.row_ref, s32[8,8,128]{2,1,0:T(8,128)S(1)} %bitcast.8, s32[32]{0:T(128)S(1)} %bitcast.9, ...), custom_call_target="tpu_custom_call" | custom-call | flops 12884901888 | bytes 16777216 | tf_op jit(solution)/shard_map/islands/pallas_call | solution.py:365
  67.8 0.0 copy-start.5
  67.9 6.9 %all-to-all-start = ((bf16[32,2,128,128]{3,2,1,0:T(8,128)(2,1)}), bf16[32,2,128,128]{3,2,1,0:T(8,128)(2,1)S(1)}, u32[]{:S(2)}, u32[]{:S(2)}) async-start(bf16[32,2,128,128]{3,2,1,0:T(8,128)(2,1)} %get-tuple-element.5), calls=%async_computation | async-start | bytes 4194304 | tf_op jit(solution)/shard_map/all_to_all | solution.py:450
  74.7 0.0 copy-done.5
  74.7 0.6 reduce_sum.9
  76.0 0.0 copy-start.4
  76.0 2.8 %multiply_sine_fusion = (f32[512,288]{1,0:T(8,128)S(1)}, f32[512,288]{1,0:T(8,128)S(1)}, f32[512,288]{1,0:T(8,128)S(1)}) fusion(f32[512]{0:T(512)S(1)} %convert_multiply_fusion, f32[288]{0:T(512)S(1)} %subtract_multiply_fusion), kind=kLoop, calls=%fused_computation.3 | loop fusion | flops 294912 | bytes 1772672 | tf_op jit(solution)/shard_map/sin | solution.py:402
  78.9 0.5 fusion.k_ref
  79.4 0.0 copy-done.4
  79.4 10.7 %fdf.1 = bf16[2,512,4,1024]{3,2,1,0:T(4,128)(2,1)} custom-call(bf16[1024,576]{1,0:T(8,128)(2,1)S(1)} %fusion.k_ref, bf16[4,2,4,576,128]{4,3,2,1,0:T(8,128)(2,1)S(1)} %bitcast.10), custom_call_target="tpu_custom_call" | custom-call | flops 4831838208 | bytes 14680064 | tf_op jit(solution)/shard_map/fdf/pallas_call | solution.py:424
  90.1 12.9 %all-to-all-done = bf16[32,2,128,128]{3,2,1,0:T(8,128)(2,1)S(1)} async-done(((bf16[32,2,128,128]{3,2,1,0:T(8,128)(2,1)}), bf16[32,2,128,128]{3,2,1,0:T(8,128)(2,1)S(1)}, u32[]{:S(2)}, u32[]{:S(2)}) %all-to-all-start) | async-done | bytes 2097184 | tf_op jit(solution)/shard_map/all_to_all | solution.py:450
  103.0 2.5 %bitcast_convert_fusion = f32[1,32,2,128,128]{4,3,2,1,0:T(8,128)} fusion(bf16[32,2,128,128]{3,2,1,0:T(8,128)(2,1)S(1)} %all-to-all-done), kind=kLoop, calls=%fused_computation.2 | loop fusion | flops 1048576 | bytes 6291456 | tf_op jit(solution)/shard_map/broadcast_in_dim | solution.py:451
  (5 shorter events, 0.1 us)
Async XLA Ops:
  0.6 1.5 %copy-start = (s32[8,4,1024]{2,1,0:T(4,128)S(1)}, s32[8,4,1024]{2,1,0:T(4,128)}, u32[]{:S(2)}) copy-start(s32[8,4,1024]{2,1,0:T(4,128)} %param.7) | copy-start | bytes 393220
  2.2 1.3 %copy-start.1 = (bf16[2,72,4,1024]{3,2,1,0:T(4,128)(2,1)S(1)}, bf16[2,72,4,1024]{3,2,1,0:T(4,128)(2,1)}, u32[]{:S(2)}) copy-start(bf16[2,72,4,1024]{3,2,1,0:T(4,128)(2,1)} %stokes_ref.1) | copy-start | bytes 3538948
  3.5 0.9 copy-start.2
  4.4 0.7 copy-start.3
  67.8 6.9 %copy-start.5 = (f32[288]{0:T(512)S(1)}, f32[288]{0:T(512)}, u32[]{:S(2)}) copy-start(f32[288]{0:T(512)} %param.6) | copy-start | bytes 3460
  67.9 35.2 %all-to-all-start = ((bf16[32,2,128,128]{3,2,1,0:T(8,128)(2,1)}), bf16[32,2,128,128]{3,2,1,0:T(8,128)(2,1)S(1)}, u32[]{:S(2)}, u32[]{:S(2)}) async-start(bf16[32,2,128,128]{3,2,1,0:T(8,128)(2,1)} %get-tuple-element.5), calls=%async_computation | async-start | bytes 4194304 | tf_op jit(solution)/shard_map/all_to_all | solution.py:450
  76.0 3.4 %copy-start.4 = (bf16[4,8,576,128]{3,2,1,0:T(8,128)(2,1)S(1)}, bf16[4,8,576,128]{3,2,1,0:T(8,128)(2,1)}, u32[]{:S(2)}) copy-start(bf16[4,8,576,128]{3,2,1,0:T(8,128)(2,1)} %get-tuple-element.4) | copy-start | bytes 14155780

commit v3 on v2

v3 whole, which is shorter than its diff:
```python
import functools
import jax
import jax.numpy as jnp
from jax import lax
from jax.sharding import PartitionSpec as P
from jax.experimental import pallas as pl
from jax.experimental.pallas import tpu as pltpu

NC = 8
DEPTHS = 2048
STEP = 2.5
BLK = 128
LAG = 2
MESH = pl.DeviceIdType.MESH
GAIN = 0.3
LOW = 64

def gather(x, idx):
    return jnp.take_along_axis(x, idx, axis=1, mode="promise_in_bounds")


def full(row):
    return jnp.broadcast_to(row, (8, 128))


def make_tables(chans, column_ref, row_ref, t, near, spread):
    mean = jnp.sum(row_ref[...], axis=1, keepdims=True) / (2 * chans)
    lane = lax.broadcasted_iota(jnp.int32, (8, 128), 1)
    low = lane < LOW
    depth = jnp.where(low, lane, (lane - LOW) * LOW - DEPTHS // 2).astype(jnp.float32) * STEP
    plain = lane.astype(jnp.float32) * STEP

    def rows(g, _):
        twice = 2.0 * (column_ref[pl.ds(pl.multiple_of(g * 8, 8), 8), :] - mean)
        angle = twice * depth
        parts = []
        for mask in (low, ~low):
            for value in (jnp.cos(angle), jnp.sin(angle)):
                value = jnp.where(mask, value, 0.0)
                top = value.astype(jnp.bfloat16)
                parts.append(jnp.concatenate([top, (value - top.astype(jnp.float32)).astype(jnp.bfloat16)], axis=1))
        t[pl.ds(pl.multiple_of(g * 32, 32), 32), :] = jnp.concatenate(parts, axis=0)
        angle = twice * plain
        near[0, pl.ds(pl.multiple_of(g * 8, 8), 8), :] = jnp.cos(angle)
        near[1, pl.ds(pl.multiple_of(g * 8, 8), 8), :] = jnp.sin(angle)
        return 0

    lax.fori_loop(0, chans // 8, rows, 0)
    twice = 2.0 * (row_ref[:, :chans] - mean)
    angle = twice * (lax.broadcasted_iota(jnp.int32, (16, chans), 0).astype(jnp.float32) * (128 * STEP))
    cosine, sine = jnp.cos(angle), jnp.sin(angle)
    dot = functools.partial(jnp.dot, precision=lax.Precision.HIGHEST, preferred_element_type=jnp.float32)
    spread[0] = (dot(cosine, near[0]) - dot(sine, near[1])) / chans
    spread[1] = -(dot(sine, near[0]) + dot(cosine, near[1])) / chans


def make_synthesis(chans, row_ref, first, kt, ck, sk):
    total = 2 * chans
    depths = kt.shape[0] // 2
    mean = jnp.sum(row_ref[...], axis=1, keepdims=True) / total
    twice = 2.0 * (row_ref[...] - mean)
    fine = twice * (lax.broadcasted_iota(jnp.int32, (LOW, total), 0).astype(jnp.float32) * STEP)
    ck[...] = jnp.cos(fine)
    sk[...] = jnp.sin(fine)
    steps = lax.broadcasted_iota(jnp.int32, (8, total), 0) * LOW + (first - DEPTHS // 2)
    coarse = twice * (steps.astype(jnp.float32) * STEP)
    cosine, sine = jnp.cos(coarse), jnp.sin(coarse)
    is_q = lax.broadcasted_iota(jnp.int32, (16, total), 1) < chans
    for h in range(depths // LOW):
        ch, sh = cosine[h:h+1], sine[h:h+1]
        for l in range(0, LOW, 16):
            cl, sl = ck[l:l+16, :], sk[l:l+16, :]
            c = (ch * cl - sh * sl) / chans
            s = (sh * cl + ch * sl) / chans
            at = h * LOW + l
            kt[at:at+16, :] = jnp.where(is_q, c, s).astype(jnp.bfloat16)
            kt[depths+at:depths+at+16, :] = jnp.where(is_q, -s, c).astype(jnp.bfloat16)


def synthesize(source, tile, tiles, kt, res, mixed, stage):
    rows, depths = 2 * tiles, kt.shape[0]
    for pair in range(2):
        a = res[source, tile * 2 + pair]
        b = res[source, tiles * 2 + tile * 2 + pair]
        block = jnp.concatenate([a[:, :64], b[:, :64], a[:, 64:], b[:, 64:]], axis=1)
        for first in range(0, depths, 256):
            part = jnp.dot(kt[first:first + 256, :], block, preferred_element_type=jnp.float32)
            for row in range(2):
                mixed[pl.ds(first * rows + pair * 2 + row, 256, rows), :] = part[:, row * 128:(row + 1) * 128]
    stage[...] = mixed[...].astype(jnp.bfloat16).reshape(stage.shape)


def clean_tile(chans, pair, half, rows, data, peaks, t, spread, out_ref, oh, e4, ec, es, joint):
    groups = chans // 8
    stays, moves = pair * 2 + half, pair * 2 + 1 - half
    here = (lax.broadcasted_iota(jnp.int32, (8, 128), 1) < 64) == (half == 0)

    def merged(ref, base):
        kept = ref[pl.ds(base + stays, 8, rows), :]
        moved = ref[pl.ds(base + moves, 8, rows), :]
        return jnp.where(here, kept, pltpu.roll(moved, 64, 1))

    picks = merged(peaks, 0)
    lo = picks & (LOW - 1)
    hi = (picks >> 6) + LOW
    index = lax.broadcasted_iota(jnp.int32, (128, 128), 0)
    for j in range(NC):
        cols = slice(j * 128, (j + 1) * 128)
        hot = ((index == lo[j:j+1]) | (index == hi[j:j+1])).astype(jnp.bfloat16)
        oh[0:128, cols] = hot
        oh[128:256, cols] = hot
    e4[...] = jnp.dot(t[...], oh[...], preferred_element_type=jnp.float32)

    def peak(g, acc):
        q, u = merged(data.at[0], g * (8 * rows)), merged(data.at[1], g * (8 * rows))
        joint[0, g] = q
        joint[1, g] = u
        base = pl.multiple_of(g * 32, 32)
        out = []
        for j in range(NC):
            cols = slice(j * 128, (j + 1) * 128)
            cl, sl = e4[pl.ds(base, 8), cols], e4[pl.ds(base + 8, 8), cols]
            ch, sh = e4[pl.ds(base + 16, 8), cols], e4[pl.ds(base + 24, 8), cols]
            c = ch * cl - sh * sl
            s = sh * cl + ch * sl
            ec[g * NC + j] = c
            es[g * NC + j] = s
            out.append((acc[j][0] + (q * c + u * s), acc[j][1] + (u * c - q * s)))
        return tuple(out)

    zero = jnp.zeros((8, 128), jnp.float32)
    acc = lax.fori_loop(0, groups, peak, tuple((zero, zero) for _ in range(NC)))
    scale = 1.0 / chans
    vr = jnp.concatenate([jnp.sum(a[0], axis=0, keepdims=True) for a in acc], axis=0) * scale
    vi = jnp.concatenate([jnp.sum(a[1], axis=0, keepdims=True) for a in acc], axis=0) * scale
    comps = []
    for i in range(NC):
        cr = full(vr[i:i+1] * GAIN)
        ci = full(vi[i:i+1] * GAIN)
        comps.append((cr, ci))
        if i == NC - 1:
            break
        d = picks - picks[i:i+1]
        a = jnp.abs(d)
        alo, ahi = a & 127, a >> 7
        rr, ri = zero, zero
        for h in range(16):
            here = ahi == h
            rr = jnp.where(here, gather(full(spread[0, h:h+1, :]), alo), rr)
            ri = jnp.where(here, gather(full(spread[1, h:h+1, :]), alo), ri)
        ri = jnp.where(d < 0, -ri, ri)
        vr = vr - (cr * rr - ci * ri)
        vi = vi - (cr * ri + ci * rr)

    def model(pair, _):
        real, imag = [], []
        for part in range(2):
            g = pair * 2 + part
            q, u = joint[0, g], joint[1, g]
            mr, mi = zero, zero
            for j in range(NC):
                c, s = ec[g * NC + j], es[g * NC + j]
                cr, ci = comps[j]
                mr = mr + (cr * c - ci * s)
                mi = mi + (cr * s + ci * c)
            real.append(q - mr)
            imag.append(u - mi)
        out_ref[pl.ds(pl.multiple_of(pair * 16, 16), 16), :] = jnp.concatenate(real, axis=0).astype(jnp.bfloat16)
        out_ref[pl.ds(pl.multiple_of(chans + pair * 16, 16), 16), :] = jnp.concatenate(imag, axis=0).astype(jnp.bfloat16)
        return 0

    lax.fori_loop(0, groups // 2, model, 0)


def island_kernel(chans, stokes_ref, column_ref, row_ref, peaks_ref, owner_ref, w_ref, out_ref, got_ref,
                  raw, data, res, w, fit, sent, t, near, spread, kt, ck, sk, peaks, joint_peaks, mixed, stage, oh, e4, ec, es, joint, chosen,
                  own, sa, ra, sn, rn, sf, rf, so, ow, op, sw, rw, sc, rc, sd, rd, od):
    count, skies = lax.axis_size("freq"), lax.axis_size("sky")
    me = lax.axis_index("freq")
    sky = lax.axis_index("sky")
    x, z, core = sky // 8, sky // 2 % 4, sky % 2
    rows = stokes_ref.shape[2]
    tiles = stokes_ref.shape[3] // (count * 128)
    chunks = rows * tiles
    halfway = chunks // 2
    local = stokes_ref.shape[1]
    half = chans
    left, right, far = [lax.rem(me + k, count) for k in (count - 1, 1, 2)]

    def at_x(k):
        return {"sky": lax.rem(x + k, 4) * 8 + z * 2 + core}

    def at_z(k):
        return {"sky": x * 8 + lax.rem(z + k, 4) * 2 + core}

    other = {"sky": sky + 1 - 2 * core}

    barrier = pltpu.get_barrier_semaphore()
    for k in range(1, 4):
        pl.semaphore_signal(barrier, inc=1, device_id={"freq": lax.rem(me + k, count)}, device_id_type=MESH)

    def greet(k, _):
        pl.semaphore_signal(barrier, inc=1, device_id={"sky": lax.rem(sky + k, skies)}, device_id_type=MESH)
        return 0

    lax.fori_loop(1, skies, greet, 0)
    pl.semaphore_wait(barrier, count + skies - 2)

    def columns(owner, tile):
        return pl.ds(pl.multiple_of((owner * tiles + tile) * 128, 128), 128)

    def part(tile, k):
        peer = lax.rem(me + k, count)
        return pltpu.make_async_remote_copy(
            src_ref=stokes_ref.at[:, :, :, columns(peer, tile)], dst_ref=raw.at[tile, me],
            send_sem=sa.at[tile, k], recv_sem=ra.at[tile, k], device_id={"freq": peer}, device_id_type=MESH)

    def arrived(tile, k):
        source = lax.rem(me + count - k, count)
        return pltpu.make_async_remote_copy(
            src_ref=stokes_ref.at[:, :, :, columns(me, tile)], dst_ref=raw.at[tile, source],
            send_sem=sa.at[tile, k], recv_sem=ra.at[tile, k], device_id={"freq": source}, device_id_type=MESH)

    def kept(tile):
        return pltpu.make_async_copy(stokes_ref.at[:, :, :, columns(me, tile)], raw.at[tile, me], own.at[tile])

    for tile in range(tiles):
        kept(tile).start()
        for k in (1, 3, 2):
            part(tile, k).start()
    mine = pl.ds(pl.multiple_of(me * (tiles * 128), 128), tiles * 128)
    pltpu.make_async_copy(peaks_ref.at[:, :, mine], peaks, op).start()
    pltpu.make_async_copy(w_ref.at[0], w.at[x, z, core], ow).start()
    pltpu.make_async_copy(w_ref.at[0], w.at[x, z, core], ow).wait()

    def w_first(h, k, source=None):
        along_x = h == 0
        lines = pl.ds(h * half, half)
        piece = w.at[x, z, core, lines]
        if source is not None:
            piece = w.at[lax.rem(x + 4 - k, 4), z, core, lines] if along_x else w.at[x, lax.rem(z + 4 - k, 4), core, lines]
        return pltpu.make_async_remote_copy(
            src_ref=piece, dst_ref=piece, send_sem=sw.at[0, h, k], recv_sem=rw.at[0, h, k],
            device_id=at_x(k) if along_x else at_z(k), device_id_type=MESH)

    def w_second(h, k, source=None):
        along_x = h == 1
        lines = pl.ds(h * half, half)
        back = k if source is not None else 4
        if along_x:
            piece = w.at[lax.rem(x + 4 - back + (4 if back == 4 else 0), 4), :, core, lines]
        else:
            piece = w.at[:, lax.rem(z + 4 - back + (4 if back == 4 else 0), 4), core, lines]
        return pltpu.make_async_remote_copy(
            src_ref=piece, dst_ref=piece, send_sem=sw.at[1, h, k], recv_sem=rw.at[1, h, k],
            device_id=at_x(k) if along_x else at_z(k), device_id_type=MESH)

    def w_third(which):
        piece = w.at[:, :, which]
        return pltpu.make_async_remote_copy(
            src_ref=piece, dst_ref=piece, send_sem=sc, recv_sem=rc, device_id=other, device_id_type=MESH)

    for h in range(2):
        for k in range(1, 4):
            w_first(h, k).start()

    def slot(o, _):
        first, second = jnp.int32(-1), jnp.int32(-1)
        for b in reversed(range(owner_ref.shape[0])):
            hit = owner_ref[b] == o
            second = jnp.where(hit, first, second)
            first = jnp.where(hit, b, first)
        chosen[o * 2] = first
        chosen[o * 2 + 1] = second
        return 0

    lax.fori_loop(0, skies, slot, 0)
    make_tables(chans, column_ref, row_ref, t, near, spread)

    def to_neighbour(c, way, source):
        return pltpu.make_async_remote_copy(
            src_ref=res.at[source, c], dst_ref=res.at[source, c],
            send_sem=sn.at[c, way], recv_sem=rn.at[c, way],
            device_id={"freq": right if way == 0 else left}, device_id_type=MESH)

    def onward(c, way, source):
        piece = res.at[source, c, pl.ds(way * half, half)]
        return pltpu.make_async_remote_copy(
            src_ref=piece, dst_ref=piece, send_sem=sf.at[c, way], recv_sem=rf.at[c, way],
            device_id={"freq": right if way == 0 else left}, device_id_type=MESH)

    def relay(c):
        to_neighbour(c, 0, left).wait_recv()
        onward(c, 0, left).start()
        to_neighbour(c, 1, right).wait_recv()
        onward(c, 1, right).start()

    def fit_chunk(source, c):
        part, tile, pair = c // halfway, c // 2 % tiles, c % 2
        b = pair * (2 * count * tiles) + source * tiles + tile
        after = b + count * tiles
        o, p = owner_ref[b], owner_ref[after]
        both = jnp.concatenate([w[o >> 3, (o >> 1) & 3, o & 1], w[p >> 3, (p >> 1) & 3, p & 1]], axis=1)
        value = lax.dot_general(res[source, c], both, (((0,), (0,)), ((), ())), preferred_element_type=jnp.float32)
        terms = value.shape[1] // 2
        fit[part, b] = value[:64, :terms].astype(jnp.bfloat16)
        fit[part, after] = value[64:, terms:].astype(jnp.bfloat16)

    def fit_some(sources, first, last):
        def some(c, _):
            for source in sources:
                fit_chunk(source, c)
            return 0
        lax.fori_loop(first, last, some, 0)

    def fit_far(first, last):
        def some(c, _):
            onward(c, 0, far).wait_recv()
            onward(c, 1, far).wait_recv()
            fit_chunk(far, c)
            return 0
        lax.fori_loop(first, last, some, 0)

    def result(part, k, source):
        peer = lax.rem(sky + k, skies)
        return pltpu.make_async_remote_copy(
            src_ref=sent.at[part, peer], dst_ref=got_ref.at[source, :, pl.ds(part * 64, 64)],
            send_sem=sd.at[part, k], recv_sem=rd.at[part, k], device_id={"sky": peer}, device_id_type=MESH)

    def kept_result(part):
        return pltpu.make_async_copy(sent.at[part, sky], got_ref.at[sky, :, pl.ds(part * 64, 64)], od.at[part])

    def send_results(part):
        def fill(o, _):
            for rank in range(2):
                b = chosen[o * 2 + rank]
                value = fit[part, jnp.maximum(b, 0)]
                sent[part, o, rank] = jnp.where(b >= 0, value, jnp.zeros_like(value))
            return 0

        def send(k, _):
            result(part, k, sky).start()
            return 0

        lax.fori_loop(0, skies, fill, 0)
        lax.fori_loop(1, skies, send, 0)
        kept_result(part).start()

    pltpu.make_async_copy(peaks_ref.at[:, :, mine], peaks, op).wait()

    def step(c, _):
        part, tile, pair = c // halfway, c // 2 % tiles, c % 2

        @pl.when((pair == 0) & (part == 0))
        def _():
            kept(tile).wait()
            for k in (1, 3, 2):
                arrived(tile, k).wait_recv()
            for source in range(count):
                for plane in range(2):
                    block = raw[tile, source, plane].reshape(local * rows, 128)
                    data[tile, plane, source * local * rows:(source + 1) * local * rows, :] = block.astype(jnp.float32)
            joint_peaks[tile] = peaks[:, :, pl.ds(pl.multiple_of(tile * 128, 128), 128)].reshape(NC * rows, 128)

        clean_tile(chans, pair, part, rows, data.at[tile], joint_peaks.at[tile], t, spread, res.at[me, c], oh, e4, ec, es, joint)
        to_neighbour(c, 0, me).start()
        to_neighbour(c, 1, me).start()

        @pl.when(c >= LAG)
        def _():
            relay(c - LAG)

        @pl.when(c == 1)
        def _():
            for h in range(2):
                for k in range(1, 4):
                    w_first(h, k, True).wait_recv()
            for h in range(2):
                for k in range(1, 4):
                    w_second(h, k).start()
            make_synthesis(chans, row_ref, me * (kt.shape[0] // 2), kt, ck, sk)

        @pl.when(c == 4)
        def _():
            for h in range(2):
                for k in range(1, 4):
                    w_second(h, k, True).wait_recv()
            w_third(core).start()

        @pl.when(c == 5)
        def _():
            w_third(1 - core).wait_recv()
            fit_some((me,), 0, halfway)
            fit_some((left, right), 0, halfway - 1)

        @pl.when(c == 6)
        def _():
            fit_some((left, right), halfway - 1, halfway)
            fit_far(0, halfway)
            send_results(0)

        return 0

    lax.fori_loop(0, chunks, step, 0)
    fit_some((me,), halfway, chunks)
    relay(chunks - 2)
    fit_some((left, right), halfway, chunks - 1)
    relay(chunks - 1)
    fit_far(halfway, chunks - 1)
    fit_some((left, right), chunks - 1, chunks)
    fit_far(chunks - 1, chunks)
    send_results(1)

    def put(u):
        cols = pl.ds(pl.multiple_of(u * 128, 128), 128)
        return pltpu.make_async_copy(stage.at[u % 2], out_ref.at[:, :, :, cols], so.at[u])

    def unit(u, _):
        @pl.when(u >= 2)
        def _():
            put(u - 2).wait()

        synthesize(u // tiles, u % tiles, tiles, kt, res, mixed, stage.at[u % 2])
        put(u).start()
        return 0

    lax.fori_loop(0, count * tiles, unit, 0)
    put(count * tiles - 2).wait()
    put(count * tiles - 1).wait()

    for tile in range(tiles):
        for k in (1, 3, 2):
            part(tile, k).wait_send()
    for h in range(2):
        for k in range(1, 4):
            w_first(h, k).wait_send()
            w_second(h, k).wait_send()
    w_third(core).wait_send()

    def finish(c, _):
        to_neighbour(c, 0, me).wait_send()
        to_neighbour(c, 1, me).wait_send()
        onward(c, 0, left).wait_send()
        onward(c, 1, right).wait_send()
        return 0

    lax.fori_loop(0, chunks, finish, 0)
    for which in range(2):
        kept_result(which).wait()

        def results(k, _):
            result(which, k, lax.rem(sky + skies - k, skies)).wait_recv()
            result(which, k, sky).wait_send()
            return 0

        lax.fori_loop(1, skies, results, 0)


def islands(stokes, lam2, peaks, owners, weights, freq_count, sky_count):
    chans, local, rows, columns = lam2.shape[0], stokes.shape[1], stokes.shape[2], stokes.shape[3]
    groups = chans // 8
    tiles = columns // (freq_count * 128)
    chunks = rows * tiles
    terms = weights.shape[2]
    depths = DEPTHS // freq_count
    dma = pltpu.SemaphoreType.DMA
    vmem = pl.BlockSpec(memory_space=pltpu.VMEM)
    smem = pl.BlockSpec(memory_space=pltpu.SMEM)
    hbm = pl.BlockSpec(memory_space=pl.ANY)
    f32, bf16 = jnp.float32, jnp.bfloat16
    return pl.pallas_call(
        functools.partial(island_kernel, chans),
        in_specs=[hbm, vmem, vmem, hbm, smem, hbm],
        out_specs=[hbm, hbm],
        out_shape=[
            jax.ShapeDtypeStruct((2, depths, rows, columns), bf16),
            jax.ShapeDtypeStruct((sky_count, 2, BLK, terms), bf16),
        ],
        scratch_shapes=[
            pltpu.VMEM((tiles, freq_count, 2, local, rows, 128), bf16),
            pltpu.VMEM((tiles, 2, chans * rows, 128), f32),
            pltpu.VMEM((freq_count, chunks, 2 * chans, 128), bf16),
            pltpu.VMEM((4, 4, 2, 2 * chans, terms), bf16),
            pltpu.VMEM((2, freq_count * chunks, 64, terms), bf16),
            pltpu.VMEM((2, sky_count, 2, 64, terms), bf16),
            pltpu.VMEM((4 * chans, 256), bf16),
            pltpu.VMEM((2, chans, 128), f32),
            pltpu.VMEM((2, 16, 128), f32),
            pltpu.VMEM((2 * depths, 2 * chans), bf16),
            pltpu.VMEM((LOW, 2 * chans), f32),
            pltpu.VMEM((LOW, 2 * chans), f32),
            pltpu.VMEM((NC, rows, tiles * 128), jnp.int32),
            pltpu.VMEM((tiles, NC * rows, 128), jnp.int32),
            pltpu.VMEM((2 * depths * rows, 128), f32),
            pltpu.VMEM((2, 2, depths, rows, 128), bf16),
            pltpu.VMEM((256, NC * 128), bf16),
            pltpu.VMEM((4 * chans, NC * 128), f32),
            pltpu.VMEM((groups * NC, 8, 128), f32),
            pltpu.VMEM((groups * NC, 8, 128), f32),
            pltpu.VMEM((2, groups, 8, 128), f32),
            pltpu.SMEM((sky_count * 2,), jnp.int32),
            dma((tiles,)), dma((tiles, 4)), dma((tiles, 4)),
            dma((chunks, 2)), dma((chunks, 2)), dma((chunks, 2)), dma((chunks, 2)), dma((freq_count * tiles,)),
            dma, dma, dma((2, 2, 4)), dma((2, 2, 4)), dma, dma,
            dma((2, sky_count)), dma((2, sky_count)), dma((2,)),
        ],
        compiler_params=pltpu.CompilerParams(collective_id=0, has_side_effects=True, vmem_limit_bytes=60 << 20),
        cost_estimate=pl.CostEstimate(flops=6 << 32, bytes_accessed=24 << 20, transcendentals=0),
        name="islands",
    )(stokes, lam2.reshape(chans, 1), jnp.concatenate([lam2, lam2]).reshape(1, 2 * chans), peaks, owners, weights)


def shards(stokes, lam2, peaks, island_owner, fit_matrix):
    freq_count, sky_count = lax.axis_size("freq"), lax.axis_size("sky")
    residual_fdf, got = islands(stokes, lam2, peaks, island_owner[:, 0], fit_matrix, freq_count, sky_count)
    return residual_fdf, got.astype(jnp.float32)[None]


def solution(mesh):
    in_specs = (
        P(None, "freq", "sky", None),
        P(),
        P(None, "sky", None),
        P("sky", None),
        P("sky", None, "freq"),
    )
    out_specs = (P(None, "freq", "sky", None), P("sky", None, None, None, "freq"))
    return jax.shard_map(shards, mesh=mesh, in_specs=in_specs, out_specs=out_specs, check_vma=False)
```

time: 106 us -> 106 us (level); the launches traced: 106 us -> 104 us
  Pallas kernels: 73.5 us -> 88.8 us
  waiting for transfers between devices: 12.9 us -> 0 us
  starting transfers between devices: 6.85 us -> 0 us
  local copies, waits for them, and re-layouts: 4.39 us -> 10.1 us
  other arithmetic: 6.51 us -> 4.96 us
    pallas_call x1, Pallas kernels: 62.8 us -> 88.8 us  [islands(): pl.pallas_call(functools.partial(island_kernel, chans), in_specs=[hbm, vm...]
    all_to_all x1 -> x0, waiting for transfers between devices: 12.9 us -> none  [shards(): got = lax.all_to_all(sent, 'sky', split_axis=0, concat_axis=0, tiled=True)]
    pallas_call x1 -> x0, Pallas kernels: 10.7 us -> none  [fdf(): pl.pallas_call(fdf_kernel, grid=(count * tiles,), in_specs=[pl.BlockSpec(...]
    all_to_all x1 -> x0, starting transfers between devices: 6.85 us -> none  [shards(): got = lax.all_to_all(sent, 'sky', split_axis=0, concat_axis=0, tiled=True)]
    unnamed x12 -> x1, local copies, waits for them, and re-layouts: 2.85 us -> 8.05 us
    sin x1 -> x0, other arithmetic: 2.83 us -> none  [synthesis(): cosine, sine = (jnp.cos(angle), jnp.sin(angle))]
    broadcast_in_dim x1, other arithmetic: 2.54 us -> 4.13 us  [shards(): return (residual_fdf, got.astype(jnp.float32)[None])]
  transfers between devices with their start and end apart: 1 -> 0, of which waited for: 1 -> 0; matrix products, arithmetic and copies ran while one was open for 4% -> 0% of each run, Pallas kernels for 10% -> 0%
where the time goes in v3:
time: 106 us; the launch traced here: 104 us
  Pallas kernels  88.8 us (84%)
  local copies, waits for them, and re-layouts  10.1 us (10%)
  other arithmetic  4.96 us (5%)
    pallas_call x1, Pallas kernels, islands(): pl.pallas_call(functools.partial(island_kernel, chans), in_specs=[hbm, vm...  88.8 us
    unnamed x1, local copies, waits for them, and re-layouts  8.05 us
    broadcast_in_dim x1, other arithmetic, shards(): return (residual_fdf, got.astype(jnp.float32)[None])  4.13 us

profile of v3, /device:TPU:1, one launch (start us, length us, event | category | flops | bytes accessed | tf_op | source)
XLA Modules:
  0.0 104.4 jit_solution(3842448049771935904)
XLA Ops:
  0.6 0.8 pad_maximum_fusion
  1.5 0.6 reshape.11.row_ref
  2.0 1.4 %reshape.13.column_ref = f32[288,1]{1,0:T(8,128)} reshape(f32[288]{0:T(512)} %param.6) | data formatting | bytes 2304 | tf_op jit(solution)/shard_map/reshape | solution.py:510
  3.5 88.8 %islands.1 = (bf16[2,512,4,1024]{3,2,1,0:T(4,128)(2,1)}, bf16[32,2,128,128]{3,2,1,0:T(8,128)(2,1)}) custom-call(bf16[2,72,4,1024]{3,2,1,0:T(4,128)(2,1)} %stokes_ref.1, f32[288,1]{1,0:T(8,128)} %reshape.13.column_ref, f32[1,576]{1,0:T(1,128)} %reshape.11.row_ref, s32[8,4,1024]{2,1,0:T(4,128)} %peaks_ref.1, s32[32]{0:T(128)} %bitcast.4, ...), custom_call_target="tpu_custom_call" | custom-call | flops 25769803776 | bytes 25165824 | tf_op jit(solution)/shard_map/islands/pallas_call | solution.py:471
  92.3 4.1 %bitcast_convert_fusion = f32[1,32,2,128,128]{4,3,2,1,0:T(8,128)} fusion(bf16[32,2,128,128]{3,2,1,0:T(8,128)(2,1)} %get-tuple-element.5), kind=kLoop, calls=%fused_computation | loop fusion | flops 1048576 | bytes 6291456 | tf_op jit(solution)/shard_map/broadcast_in_dim | solution.py:516
  96.4 8.1 %copy.9 = bf16[2,512,4,1024]{3,2,1,0:T(4,128)(2,1)} copy(bf16[2,512,4,1024]{3,2,1,0:T(4,128)(2,1)} %get-tuple-element.8) | data formatting | bytes 16777216

commit v4 on v3

--- a/solution.py
+++ b/solution.py
@@ -23,15 +23,17 @@
     return jnp.broadcast_to(row, (8, 128))
 
 
-def make_tables(chans, column_ref, row_ref, t, near, spread):
-    mean = jnp.sum(row_ref[...], axis=1, keepdims=True) / (2 * chans)
+def make_tables(chans, row_ref, t, near, spread):
+    mean = jnp.sum(row_ref[...], axis=1, keepdims=True) / chans
+    along = jnp.broadcast_to(row_ref[...] - mean, (8, chans))
+    place = lax.broadcasted_iota(jnp.int32, (8, chans), 1) - lax.broadcasted_iota(jnp.int32, (8, chans), 0)
     lane = lax.broadcasted_iota(jnp.int32, (8, 128), 1)
     low = lane < LOW
     depth = jnp.where(low, lane, (lane - LOW) * LOW - DEPTHS // 2).astype(jnp.float32) * STEP
     plain = lane.astype(jnp.float32) * STEP
 
     def rows(g, _):
-        twice = 2.0 * (column_ref[pl.ds(pl.multiple_of(g * 8, 8), 8), :] - mean)
+        twice = 2.0 * jnp.sum(jnp.where(place == g * 8, along, 0.0), axis=1, keepdims=True)
         angle = twice * depth
         parts = []
         for mask in (low, ~low):
@@ -46,7 +48,7 @@
         return 0
 
     lax.fori_loop(0, chans // 8, rows, 0)
-    twice = 2.0 * (row_ref[:, :chans] - mean)
+    twice = 2.0 * (row_ref[...] - mean)
     angle = twice * (lax.broadcasted_iota(jnp.int32, (16, chans), 0).astype(jnp.float32) * (128 * STEP))
     cosine, sine = jnp.cos(angle), jnp.sin(angle)
     dot = functools.partial(jnp.dot, precision=lax.Precision.HIGHEST, preferred_element_type=jnp.float32)
@@ -57,8 +59,9 @@
 def make_synthesis(chans, row_ref, first, kt, ck, sk):
     total = 2 * chans
     depths = kt.shape[0] // 2
-    mean = jnp.sum(row_ref[...], axis=1, keepdims=True) / total
+    mean = jnp.sum(row_ref[...], axis=1, keepdims=True) / chans
     twice = 2.0 * (row_ref[...] - mean)
+    twice = jnp.concatenate([twice, twice], axis=1)
     fine = twice * (lax.broadcasted_iota(jnp.int32, (LOW, total), 0).astype(jnp.float32) * STEP)
     ck[...] = jnp.cos(fine)
     sk[...] = jnp.sin(fine)
@@ -77,17 +80,37 @@
             kt[depths+at:depths+at+16, :] = jnp.where(is_q, -s, c).astype(jnp.bfloat16)
 
 
-def synthesize(source, tile, tiles, kt, res, mixed, stage):
-    rows, depths = 2 * tiles, kt.shape[0]
-    for pair in range(2):
-        a = res[source, tile * 2 + pair]
-        b = res[source, tiles * 2 + tile * 2 + pair]
+def fdf_kernel(k_ref, res_ref, out_ref, mixed):
+    rows, depths = out_ref.shape[2], k_ref.shape[0]
+    for pair in range(rows // 2):
+        a, b = res_ref[0, 0, 0, pair], res_ref[0, 1, 0, pair]
         block = jnp.concatenate([a[:, :64], b[:, :64], a[:, 64:], b[:, 64:]], axis=1)
         for first in range(0, depths, 256):
-            part = jnp.dot(kt[first:first + 256, :], block, preferred_element_type=jnp.float32)
+            part = jnp.dot(k_ref[first:first + 256, :], block, preferred_element_type=jnp.float32)
             for row in range(2):
                 mixed[pl.ds(first * rows + pair * 2 + row, 256, rows), :] = part[:, row * 128:(row + 1) * 128]
-    stage[...] = mixed[...].astype(jnp.bfloat16).reshape(stage.shape)
+    out_ref[...] = mixed[...].astype(jnp.bfloat16).reshape(out_ref.shape)
+
+
+def fdf(kt, res, rows):
+    count, chunks, total, _ = res.shape
+    tiles = chunks // rows
+    depths = kt.shape[0]
+    columns = count * tiles * 128
+    return pl.pallas_call(
+        fdf_kernel,
+        grid=(count * tiles,),
+        in_specs=[
+            pl.BlockSpec((depths, total), lambda i: (0, 0)),
+            pl.BlockSpec((1, 2, 1, rows // 2, total, 128), lambda i: (i // tiles, 0, i % tiles, 0, 0, 0)),
+        ],
+        out_specs=pl.BlockSpec((2, depths // 2, rows, 128), lambda i: (0, 0, 0, i)),
+        out_shape=jax.ShapeDtypeStruct((2, depths // 2, rows, columns), jnp.bfloat16),
+        scratch_shapes=[pltpu.VMEM((depths * rows, 128), jnp.float32)],
+        compiler_params=pltpu.CompilerParams(vmem_limit_bytes=60 << 20),
+        cost_estimate=pl.CostEstimate(flops=2 * depths * total * rows * columns, bytes_accessed=14 << 20, transcendentals=0),
+        name="fdf",
+    )(kt, res.reshape(count, 2, tiles, rows // 2, total, 128))
 
 
 def clean_tile(chans, pair, half, rows, data, peaks, t, spread, out_ref, oh, e4, ec, es, joint):
@@ -111,10 +134,16 @@
         oh[128:256, cols] = hot
     e4[...] = jnp.dot(t[...], oh[...], preferred_element_type=jnp.float32)
 
+    def join(g, _):
+        for k in range(6):
+            joint[0, g * 6 + k] = merged(data.at[0], (g * 6 + k) * (8 * rows))
+            joint[1, g * 6 + k] = merged(data.at[1], (g * 6 + k) * (8 * rows))
+        return 0
+
+    lax.fori_loop(0, groups // 6, join, 0)
+
     def peak(g, acc):
-        q, u = merged(data.at[0], g * (8 * rows)), merged(data.at[1], g * (8 * rows))
-        joint[0, g] = q
-        joint[1, g] = u
+        q, u = joint[0, g], joint[1, g]
         base = pl.multiple_of(g * 32, 32)
         out = []
         for j in range(NC):
@@ -172,9 +201,9 @@
     lax.fori_loop(0, groups // 2, model, 0)
 
 
-def island_kernel(chans, stokes_ref, column_ref, row_ref, peaks_ref, owner_ref, w_ref, out_ref, got_ref,
-                  raw, data, res, w, fit, sent, t, near, spread, kt, ck, sk, peaks, joint_peaks, mixed, stage, oh, e4, ec, es, joint, chosen,
-                  own, sa, ra, sn, rn, sf, rf, so, ow, op, sw, rw, sc, rc, sd, rd, od):
+def island_kernel(chans, stokes_ref, row_ref, peaks_ref, owner_ref, w_ref, out_ref, kt_ref, got_ref, last_ref,
+                  raw, data, res, w, fit, sent, t, near, spread, kt, ck, sk, peaks, joint_peaks, oh, e4, ec, es, joint, chosen,
+                  own, sa, ra, sn, rn, sf, rf, so, ow, op, sw, rw, sc, rc, sd, rd, od, ok):
     count, skies = lax.axis_size("freq"), lax.axis_size("sky")
     me = lax.axis_index("freq")
     sky = lax.axis_index("sky")
@@ -275,7 +304,7 @@
         return 0
 
     lax.fori_loop(0, skies, slot, 0)
-    make_tables(chans, column_ref, row_ref, t, near, spread)
+    make_tables(chans, row_ref, t, near, spread)
 
     def to_neighbour(c, way, source):
         return pltpu.make_async_remote_copy(
@@ -289,11 +318,16 @@
             src_ref=piece, dst_ref=piece, send_sem=sf.at[c, way], recv_sem=rf.at[c, way],
             device_id={"freq": right if way == 0 else left}, device_id_type=MESH)
 
+    def keep(c, source):
+        return pltpu.make_async_copy(res.at[source, c], out_ref.at[source, c], so.at[c, source])
+
     def relay(c):
         to_neighbour(c, 0, left).wait_recv()
         onward(c, 0, left).start()
+        keep(c, left).start()
         to_neighbour(c, 1, right).wait_recv()
         onward(c, 1, right).start()
+        keep(c, right).start()
 
     def fit_chunk(source, c):
         part, tile, pair = c // halfway, c // 2 % tiles, c % 2
@@ -317,34 +351,38 @@
         def some(c, _):
             onward(c, 0, far).wait_recv()
             onward(c, 1, far).wait_recv()
+            keep(c, far).start()
             fit_chunk(far, c)
             return 0
         lax.fori_loop(first, last, some, 0)
 
-    def result(part, k, source):
+    def result(k, source):
         peer = lax.rem(sky + k, skies)
         return pltpu.make_async_remote_copy(
-            src_ref=sent.at[part, peer], dst_ref=got_ref.at[source, :, pl.ds(part * 64, 64)],
-            send_sem=sd.at[part, k], recv_sem=rd.at[part, k], device_id={"sky": peer}, device_id_type=MESH)
-
-    def kept_result(part):
-        return pltpu.make_async_copy(sent.at[part, sky], got_ref.at[sky, :, pl.ds(part * 64, 64)], od.at[part])
-
-    def send_results(part):
+            src_ref=sent.at[peer], dst_ref=got_ref.at[source],
+            send_sem=sd.at[k], recv_sem=rd.at[k], device_id={"sky": peer}, device_id_type=MESH)
+
+    def kept_result():
+        return pltpu.make_async_copy(sent.at[sky], got_ref.at[sky], od)
+
+    def fill_slots(part, slots):
         def fill(o, _):
             for rank in range(2):
                 b = chosen[o * 2 + rank]
                 value = fit[part, jnp.maximum(b, 0)]
-                sent[part, o, rank] = jnp.where(b >= 0, value, jnp.zeros_like(value))
+                slots[o, rank] = jnp.where(b >= 0, value, jnp.zeros_like(value))
             return 0
 
+        lax.fori_loop(0, skies, fill, 0)
+
+    def send_results():
         def send(k, _):
-            result(part, k, sky).start()
+            result(k, sky).start()
             return 0
 
-        lax.fori_loop(0, skies, fill, 0)
+        fill_slots(0, sent)
         lax.fori_loop(1, skies, send, 0)
-        kept_result(part).start()
+        kept_result().start()
 
     pltpu.make_async_copy(peaks_ref.at[:, :, mine], peaks, op).wait()
 
@@ -365,6 +403,7 @@
         clean_tile(chans, pair, part, rows, data.at[tile], joint_peaks.at[tile], t, spread, res.at[me, c], oh, e4, ec, es, joint)
         to_neighbour(c, 0, me).start()
         to_neighbour(c, 1, me).start()
+        keep(c, me).start()
 
         @pl.when(c >= LAG)
         def _():
@@ -379,6 +418,7 @@
                 for k in range(1, 4):
                     w_second(h, k).start()
             make_synthesis(chans, row_ref, me * (kt.shape[0] // 2), kt, ck, sk)
+            pltpu.make_async_copy(kt, kt_ref, ok).start()
 
         @pl.when(c == 4)
         def _():
@@ -397,7 +437,7 @@
         def _():
             fit_some((left, right), halfway - 1, halfway)
             fit_far(0, halfway)
-            send_results(0)
+            send_results()
 
         return 0
 
@@ -409,24 +449,7 @@
     fit_far(halfway, chunks - 1)
     fit_some((left, right), chunks - 1, chunks)
     fit_far(chunks - 1, chunks)
-    send_results(1)
-
-    def put(u):
-        cols = pl.ds(pl.multiple_of(u * 128, 128), 128)
-        return pltpu.make_async_copy(stage.at[u % 2], out_ref.at[:, :, :, cols], so.at[u])
-
-    def unit(u, _):
-        @pl.when(u >= 2)
-        def _():
-            put(u - 2).wait()
-
-        synthesize(u // tiles, u % tiles, tiles, kt, res, mixed, stage.at[u % 2])
-        put(u).start()
-        return 0
-
-    lax.fori_loop(0, count * tiles, unit, 0)
-    put(count * tiles - 2).wait()
-    put(count * tiles - 1).wait()
+    fill_slots(1, last_ref)
 
     for tile in range(tiles):
         for k in (1, 3, 2):
@@ -442,18 +465,20 @@
         to_neighbour(c, 1, me).wait_send()
         onward(c, 0, left).wait_send()
         onward(c, 1, right).wait_send()
+        for source in (me, left, right, far):
+            keep(c, source).wait()
         return 0
 
     lax.fori_loop(0, chunks, finish, 0)
-    for which in range(2):
-        kept_result(which).wait()
-
-        def results(k, _):
-            result(which, k, lax.rem(sky + skies - k, skies)).wait_recv()
-            result(which, k, sky).wait_send()
-            return 0
-
-        lax.fori_loop(1, skies, results, 0)
+    pltpu.make_async_copy(kt, kt_ref, ok).wait()
+    kept_result().wait()
+
+    def results(k, _):
+        result(k, lax.rem(sky + skies - k, skies)).wait_recv()
+        result(k, sky).wait_send()
+        return 0
+
+    lax.fori_loop(1, skies, results, 0)
 
 
 def islands(stokes, lam2, peaks, owners, weights, freq_count, sky_count):
@@ -470,11 +495,13 @@
     f32, bf16 = jnp.float32, jnp.bfloat16
     return pl.pallas_call(
         functools.partial(island_kernel, chans),
-        in_specs=[hbm, vmem, vmem, hbm, smem, hbm],
-        out_specs=[hbm, hbm],
+        in_specs=[hbm, vmem, hbm, smem, hbm],
+        out_specs=[hbm, hbm, hbm, vmem],
         out_shape=[
-            jax.ShapeDtypeStruct((2, depths, rows, columns), bf16),
-            jax.ShapeDtypeStruct((sky_count, 2, BLK, terms), bf16),
+            jax.ShapeDtypeStruct((freq_count, chunks, 2 * chans, 128), bf16),
+            jax.ShapeDtypeStruct((2 * depths, 2 * chans), bf16),
+            jax.ShapeDtypeStruct((sky_count, 2, 64, terms), bf16),
+            jax.ShapeDtypeStruct((sky_count, 2, 64, terms), bf16),
         ],
         scratch_shapes=[
             pltpu.VMEM((tiles, freq_count, 2, local, rows, 128), bf16),
@@ -482,7 +509,7 @@
             pltpu.VMEM((freq_count, chunks, 2 * chans, 128), bf16),
             pltpu.VMEM((4, 4, 2, 2 * chans, terms), bf16),
             pltpu.VMEM((2, freq_count * chunks, 64, terms), bf16),
-            pltpu.VMEM((2, sky_count, 2, 64, terms), bf16),
+            pltpu.VMEM((sky_count, 2, 64, terms), bf16),
             pltpu.VMEM((4 * chans, 256), bf16),
             pltpu.VMEM((2, chans, 128), f32),
             pltpu.VMEM((2, 16, 128), f32),
@@ -491,8 +518,6 @@
             pltpu.VMEM((LOW, 2 * chans), f32),
             pltpu.VMEM((NC, rows, tiles * 128), jnp.int32),
             pltpu.VMEM((tiles, NC * rows, 128), jnp.int32),
-            pltpu.VMEM((2 * depths * rows, 128), f32),
-            pltpu.VMEM((2, 2, depths, rows, 128), bf16),
             pltpu.VMEM((256, NC * 128), bf16),
             pltpu.VMEM((4 * chans, NC * 128), f32),
             pltpu.VMEM((groups * NC, 8, 128), f32),
@@ -500,20 +525,22 @@
             pltpu.VMEM((2, groups, 8, 128), f32),
             pltpu.SMEM((sky_count * 2,), jnp.int32),
             dma((tiles,)), dma((tiles, 4)), dma((tiles, 4)),
-            dma((chunks, 2)), dma((chunks, 2)), dma((chunks, 2)), dma((chunks, 2)), dma((freq_count * tiles,)),
+            dma((chunks, 2)), dma((chunks, 2)), dma((chunks, 2)), dma((chunks, 2)), dma((chunks, 4)),
             dma, dma, dma((2, 2, 4)), dma((2, 2, 4)), dma, dma,
-            dma((2, sky_count)), dma((2, sky_count)), dma((2,)),
+            dma((sky_count,)), dma((sky_count,)), dma, dma,
         ],
         compiler_params=pltpu.CompilerParams(collective_id=0, has_side_effects=True, vmem_limit_bytes=60 << 20),
         cost_estimate=pl.CostEstimate(flops=6 << 32, bytes_accessed=24 << 20, transcendentals=0),
         name="islands",
-    )(stokes, lam2.reshape(chans, 1), jnp.concatenate([lam2, lam2]).reshape(1, 2 * chans), peaks, owners, weights)
+    )(stokes, lam2.reshape(1, chans), peaks, owners, weights)
 
 
 def shards(stokes, lam2, peaks, island_owner, fit_matrix):
     freq_count, sky_count = lax.axis_size("freq"), lax.axis_size("sky")
-    residual_fdf, got = islands(stokes, lam2, peaks, island_owner[:, 0], fit_matrix, freq_count, sky_count)
-    return residual_fdf, got.astype(jnp.float32)[None]
+    res, kt, early, late = islands(stokes, lam2, peaks, island_owner[:, 0], fit_matrix, freq_count, sky_count)
+    late = lax.all_to_all(late, "sky", split_axis=0, concat_axis=0, tiled=True)
+    coefficients = jnp.concatenate([early, late], axis=2)
+    return fdf(kt, res, stokes.shape[2]), coefficients.astype(jnp.float32)[None]
 
 
 def solution(mesh):

time: 106 us -> 104 us (0.981)
  starting transfers between devices: 0 us -> 12.1 us
  local copies, waits for them, and re-layouts: 10.1 us -> 1.25 us
  Pallas kernels: 88.8 us -> 83 us
  waiting for transfers between devices: 0 us -> 3.48 us
  other arithmetic: 4.96 us -> 2.54 us
    pallas_call x1, Pallas kernels: 88.8 us -> 69.5 us  [islands(): pl.pallas_call(functools.partial(island_kernel, chans), in_specs=[hbm, vm...]
    pallas_call x0 -> x1, Pallas kernels: none -> 13.4 us  [fdf(): pl.pallas_call(fdf_kernel, grid=(count * tiles,), in_specs=[pl.BlockSpec(...]
    all_to_all x0 -> x1, starting transfers between devices: none -> 12.1 us  [shards(): late = lax.all_to_all(late, 'sky', split_axis=0, concat_axis=0, tiled=True)]
    unnamed x1 -> x2, local copies, waits for them, and re-layouts: 8.05 us -> 0.01 us
    broadcast_in_dim x1 -> x0, other arithmetic: 4.13 us -> none  [shards(): return (residual_fdf, got.astype(jnp.float32)[None])]
    all_to_all x0 -> x1, waiting for transfers between devices: none -> 3.48 us  [shards(): late = lax.all_to_all(late, 'sky', split_axis=0, concat_axis=0, tiled=True)]
    convert_element_type x0 -> x1, other arithmetic: none -> 2.54 us  [shards(): coefficients.astype(jnp.float32)[None]]
  transfers between devices with their start and end apart: 0 -> 1, of which waited for: 0 -> 1; matrix products, arithmetic and copies ran while one was open for 0% -> 0% of each run, Pallas kernels for 0% -> 13%
where the time goes in v4:
time: 104 us; the launch traced here: 103 us
  Pallas kernels  83 us (80%)
  starting transfers between devices  12.1 us (12%)
  waiting for transfers between devices  3.48 us (3%)
  other arithmetic  2.54 us (2%)
  local copies, waits for them, and re-layouts  1.25 us (1%)
    pallas_call x1, Pallas kernels, islands(): pl.pallas_call(functools.partial(island_kernel, chans), in_specs=[hbm, vm...  69.5 us
    pallas_call x1, Pallas kernels, fdf(): pl.pallas_call(fdf_kernel, grid=(count * tiles,), in_specs=[pl.BlockSpec(...  13.4 us
    all_to_all x1, starting transfers between devices, shards(): late = lax.all_to_all(late, 'sky', split_axis=0, concat_axis=0, tiled=True)  12.1 us
    all_to_all x1, waiting for transfers between devices, shards(): late = lax.all_to_all(late, 'sky', split_axis=0, concat_axis=0, tiled=True)  3.48 us
    convert_element_type x1, other arithmetic, shards(): coefficients.astype(jnp.float32)[None]  2.54 us
  transfers between devices with their start and end apart: 1, of which 1 were waited for; matrix products, arithmetic and copies ran while one was open for 0% of the time, Pallas kernels for 13%

profile of v4, /device:TPU:1, one launch (start us, length us, event | category | flops | bytes accessed | tf_op | source)
XLA Modules:
  0.0 103.0 jit_solution(4920402086605182226)
XLA Ops:
  0.6 1.2 %reshape.39.row_ref = f32[1,288]{1,0:T(1,128)} reshape(f32[288]{0:T(512)} %param.6) | data formatting | bytes 2304 | tf_op jit(solution)/shard_map/reshape | solution.py:535
  1.9 69.5 %islands.1 = (bf16[4,8,576,128]{3,2,1,0:T(8,128)(2,1)}, bf16[1024,576]{1,0:T(8,128)(2,1)}, bf16[32,2,64,128]{3,2,1,0:T(8,128)(2,1)}, bf16[32,2,64,128]{3,2,1,0:T(8,128)(2,1)}) custom-call(bf16[2,72,4,1024]{3,2,1,0:T(4,128)(2,1)} %stokes_ref.1, f32[1,288]{1,0:T(1,128)} %reshape.39.row_ref, s32[8,4,1024]{2,1,0:T(4,128)} %peaks_ref.1, s32[32]{0:T(128)} %bitcast.6, ...), custom_call_target="tpu_custom_call" | custom-call | flops 25769803776 | bytes 25165824 | tf_op jit(solution)/shard_map/islands/pallas_call | solution.py:496
  71.4 12.1 %all-to-all-start = ((bf16[32,2,64,128]{3,2,1,0:T(8,128)(2,1)}), bf16[32,2,64,128]{3,2,1,0:T(8,128)(2,1)S(1)}, u32[]{:S(2)}, u32[]{:S(2)}) async-start(bf16[32,2,64,128]{3,2,1,0:T(8,128)(2,1)} %get-tuple-element.9), calls=%async_computation | async-start | bytes 2097152 | tf_op jit(solution)/shard_map/all_to_all | solution.py:541
  83.5 0.0 copy-start
  83.6 13.4 %fdf.1 = bf16[2,512,4,1024]{3,2,1,0:T(4,128)(2,1)} custom-call(bf16[1024,576]{1,0:T(8,128)(2,1)} %get-tuple-element.6.k_ref, bf16[4,2,2,2,576,128]{5,4,3,2,1,0:T(8,128)(2,1)} %bitcast.7), custom_call_target="tpu_custom_call" | custom-call | flops 4831838208 | bytes 14680064 | tf_op jit(solution)/shard_map/fdf/pallas_call | solution.py:100
  97.0 3.5 %all-to-all-done = bf16[32,2,64,128]{3,2,1,0:T(8,128)(2,1)S(1)} async-done(((bf16[32,2,64,128]{3,2,1,0:T(8,128)(2,1)}), bf16[32,2,64,128]{3,2,1,0:T(8,128)(2,1)S(1)}, u32[]{:S(2)}, u32[]{:S(2)}) %all-to-all-start) | async-done | bytes 1048608 | tf_op jit(solution)/shard_map/all_to_all | solution.py:541
  100.5 0.0 copy-done
  100.5 2.5 %maximum_convert_fusion = f32[1,32,2,128,128]{4,3,2,1,0:T(8,128)} fusion(bf16[1,32,2,64,128]{4,3,2,1,0:T(8,128)(2,1)S(1)} %bitcast.4, bf16[1,32,2,64,128]{4,3,2,1,0:T(8,128)(2,1)S(1)} %bitcast.5), kind=kLoop, calls=%fused_computation | loop fusion | flops 4194304 | bytes 6291456 | tf_op jit(solution)/shard_map/convert_element_type | solution.py:543
Async XLA Ops:
  71.4 29.0 %all-to-all-start = ((bf16[32,2,64,128]{3,2,1,0:T(8,128)(2,1)}), bf16[32,2,64,128]{3,2,1,0:T(8,128)(2,1)S(1)}, u32[]{:S(2)}, u32[]{:S(2)}) async-start(bf16[32,2,64,128]{3,2,1,0:T(8,128)(2,1)} %get-tuple-element.9), calls=%async_computation | async-start | bytes 2097152 | tf_op jit(solution)/shard_map/all_to_all | solution.py:541
  83.5 16.9 %copy-start = (bf16[32,2,64,128]{3,2,1,0:T(8,128)(2,1)S(1)}, bf16[32,2,64,128]{3,2,1,0:T(8,128)(2,1)}, u32[]{:S(2)}) copy-start(bf16[32,2,64,128]{3,2,1,0:T(8,128)(2,1)} %get-tuple-element.8) | copy-start | bytes 3145732

commit v5 on v4

--- a/solution.py
+++ b/solution.py
@@ -375,14 +375,12 @@
 
         lax.fori_loop(0, skies, fill, 0)
 
-    def send_results():
+    def send_results(first, last):
         def send(k, _):
-            result(k, sky).start()
+            result(lax.rem(k * 13, skies), sky).start()
             return 0
 
-        fill_slots(0, sent)
-        lax.fori_loop(1, skies, send, 0)
-        kept_result().start()
+        lax.fori_loop(first, last, send, 0)
 
     pltpu.make_async_copy(peaks_ref.at[:, :, mine], peaks, op).wait()
 
@@ -437,15 +435,24 @@
         def _():
             fit_some((left, right), halfway - 1, halfway)
             fit_far(0, halfway)
-            send_results()
+            fill_slots(0, sent)
+            kept_result().start()
+            send_results(1, 8)
+
+        @pl.when(c == 7)
+        def _():
+            send_results(8, 16)
 
         return 0
 
     lax.fori_loop(0, chunks, step, 0)
     fit_some((me,), halfway, chunks)
+    send_results(16, 24)
     relay(chunks - 2)
     fit_some((left, right), halfway, chunks - 1)
+    send_results(24, 28)
     relay(chunks - 1)
+    send_results(28, skies)
     fit_far(halfway, chunks - 1)
     fit_some((left, right), chunks - 1, chunks)
     fit_far(chunks - 1, chunks)

time: 104 us -> 97.7 us (0.939)
  starting transfers between devices: 12.1 us -> 5.17 us
  Pallas kernels: 83 us -> 84.1 us
    all_to_all x1, starting transfers between devices: 12.1 us -> 5.17 us  [shards(): late = lax.all_to_all(late, 'sky', split_axis=0, concat_axis=0, tiled=True)]
    pallas_call x1, Pallas kernels: 69.5 us -> 70.6 us  [islands(): pl.pallas_call(functools.partial(island_kernel, chans), in_specs=[hbm, vm...]
  transfers between devices with their start and end apart: 1 -> 1, of which waited for: 1 -> 1; matrix products, arithmetic and copies ran while one was open for 0% -> 0% of each run, Pallas kernels for 13% -> 14%
where the time goes in v5:
time: 97.7 us; the launch traced here: 97.2 us
  Pallas kernels  84.1 us (86%)
  starting transfers between devices  5.17 us (5%)
  waiting for transfers between devices  3.48 us (4%)
  other arithmetic  2.54 us (3%)
  local copies, waits for them, and re-layouts  1.25 us (1%)
    pallas_call x1, Pallas kernels, islands(): pl.pallas_call(functools.partial(island_kernel, chans), in_specs=[hbm, vm...  70.6 us
    pallas_call x1, Pallas kernels, fdf(): pl.pallas_call(fdf_kernel, grid=(count * tiles,), in_specs=[pl.BlockSpec(...  13.4 us
    all_to_all x1, starting transfers between devices, shards(): late = lax.all_to_all(late, 'sky', split_axis=0, concat_axis=0, tiled=True)  5.17 us
    all_to_all x1, waiting for transfers between devices, shards(): late = lax.all_to_all(late, 'sky', split_axis=0, concat_axis=0, tiled=True)  3.48 us
    convert_element_type x1, other arithmetic, shards(): coefficients.astype(jnp.float32)[None]  2.54 us
  transfers between devices with their start and end apart: 1, of which 1 were waited for; matrix products, arithmetic and copies ran while one was open for 0% of the time, Pallas kernels for 14%

profile of v5, /device:TPU:1, one launch (start us, length us, event | category | flops | bytes accessed | tf_op | source)
XLA Modules:
  0.0 97.2 jit_solution(4408491087541118943)
XLA Ops:
  0.6 1.2 %reshape.39.row_ref = f32[1,288]{1,0:T(1,128)} reshape(f32[288]{0:T(512)} %param.6) | data formatting | bytes 2304 | tf_op jit(solution)/shard_map/reshape | solution.py:542
  1.9 70.6 %islands.1 = (bf16[4,8,576,128]{3,2,1,0:T(8,128)(2,1)}, bf16[1024,576]{1,0:T(8,128)(2,1)}, bf16[32,2,64,128]{3,2,1,0:T(8,128)(2,1)}, bf16[32,2,64,128]{3,2,1,0:T(8,128)(2,1)}) custom-call(bf16[2,72,4,1024]{3,2,1,0:T(4,128)(2,1)} %stokes_ref.1, f32[1,288]{1,0:T(1,128)} %reshape.39.row_ref, s32[8,4,1024]{2,1,0:T(4,128)} %peaks_ref.1, s32[32]{0:T(128)} %bitcast.6, ...), custom_call_target="tpu_custom_call" | custom-call | flops 25769803776 | bytes 25165824 | tf_op jit(solution)/shard_map/islands/pallas_call | solution.py:503
  72.5 5.2 %all-to-all-start = ((bf16[32,2,64,128]{3,2,1,0:T(8,128)(2,1)}), bf16[32,2,64,128]{3,2,1,0:T(8,128)(2,1)S(1)}, u32[]{:S(2)}, u32[]{:S(2)}) async-start(bf16[32,2,64,128]{3,2,1,0:T(8,128)(2,1)} %get-tuple-element.9), calls=%async_computation | async-start | bytes 2097152 | tf_op jit(solution)/shard_map/all_to_all | solution.py:548
  77.7 0.0 copy-start
  77.7 13.4 %fdf.1 = bf16[2,512,4,1024]{3,2,1,0:T(4,128)(2,1)} custom-call(bf16[1024,576]{1,0:T(8,128)(2,1)} %get-tuple-element.6.k_ref, bf16[4,2,2,2,576,128]{5,4,3,2,1,0:T(8,128)(2,1)} %bitcast.7), custom_call_target="tpu_custom_call" | custom-call | flops 4831838208 | bytes 14680064 | tf_op jit(solution)/shard_map/fdf/pallas_call | solution.py:100
  91.1 3.5 %all-to-all-done = bf16[32,2,64,128]{3,2,1,0:T(8,128)(2,1)S(1)} async-done(((bf16[32,2,64,128]{3,2,1,0:T(8,128)(2,1)}), bf16[32,2,64,128]{3,2,1,0:T(8,128)(2,1)S(1)}, u32[]{:S(2)}, u32[]{:S(2)}) %all-to-all-start) | async-done | bytes 1048608 | tf_op jit(solution)/shard_map/all_to_all | solution.py:548
  94.6 0.0 copy-done
  94.6 2.5 %maximum_convert_fusion = f32[1,32,2,128,128]{4,3,2,1,0:T(8,128)} fusion(bf16[1,32,2,64,128]{4,3,2,1,0:T(8,128)(2,1)S(1)} %bitcast.4, bf16[1,32,2,64,128]{4,3,2,1,0:T(8,128)(2,1)S(1)} %bitcast.5), kind=kLoop, calls=%fused_computation | loop fusion | flops 4194304 | bytes 6291456 | tf_op jit(solution)/shard_map/convert_element_type | solution.py:550
Async XLA Ops:
  72.5 22.1 %all-to-all-start = ((bf16[32,2,64,128]{3,2,1,0:T(8,128)(2,1)}), bf16[32,2,64,128]{3,2,1,0:T(8,128)(2,1)S(1)}, u32[]{:S(2)}, u32[]{:S(2)}) async-start(bf16[32,2,64,128]{3,2,1,0:T(8,128)(2,1)} %get-tuple-element.9), calls=%async_computation | async-start | bytes 2097152 | tf_op jit(solution)/shard_map/all_to_all | solution.py:548
  77.7 16.9 %copy-start = (bf16[32,2,64,128]{3,2,1,0:T(8,128)(2,1)S(1)}, bf16[32,2,64,128]{3,2,1,0:T(8,128)(2,1)}, u32[]{:S(2)}) copy-start(bf16[32,2,64,128]{3,2,1,0:T(8,128)(2,1)} %get-tuple-element.8) | copy-start | bytes 3145732

commit v6 on v5

--- a/solution.py
+++ b/solution.py
@@ -24,8 +24,8 @@
 
 
 def make_tables(chans, row_ref, t, near, spread):
-    mean = jnp.sum(row_ref[...], axis=1, keepdims=True) / chans
-    along = jnp.broadcast_to(row_ref[...] - mean, (8, chans))
+    mean = jnp.sum(row_ref[...].reshape(1, chans), axis=1, keepdims=True) / chans
+    along = jnp.broadcast_to(row_ref[...].reshape(1, chans) - mean, (8, chans))
     place = lax.broadcasted_iota(jnp.int32, (8, chans), 1) - lax.broadcasted_iota(jnp.int32, (8, chans), 0)
     lane = lax.broadcasted_iota(jnp.int32, (8, 128), 1)
     low = lane < LOW
@@ -48,7 +48,7 @@
         return 0
 
     lax.fori_loop(0, chans // 8, rows, 0)
-    twice = 2.0 * (row_ref[...] - mean)
+    twice = 2.0 * (row_ref[...].reshape(1, chans) - mean)
     angle = twice * (lax.broadcasted_iota(jnp.int32, (16, chans), 0).astype(jnp.float32) * (128 * STEP))
     cosine, sine = jnp.cos(angle), jnp.sin(angle)
     dot = functools.partial(jnp.dot, precision=lax.Precision.HIGHEST, preferred_element_type=jnp.float32)
@@ -59,8 +59,8 @@
 def make_synthesis(chans, row_ref, first, kt, ck, sk):
     total = 2 * chans
     depths = kt.shape[0] // 2
-    mean = jnp.sum(row_ref[...], axis=1, keepdims=True) / chans
-    twice = 2.0 * (row_ref[...] - mean)
+    mean = jnp.sum(row_ref[...].reshape(1, chans), axis=1, keepdims=True) / chans
+    twice = 2.0 * (row_ref[...].reshape(1, chans) - mean)
     twice = jnp.concatenate([twice, twice], axis=1)
     fine = twice * (lax.broadcasted_iota(jnp.int32, (LOW, total), 0).astype(jnp.float32) * STEP)
     ck[...] = jnp.cos(fine)
@@ -107,7 +107,7 @@
         out_specs=pl.BlockSpec((2, depths // 2, rows, 128), lambda i: (0, 0, 0, i)),
         out_shape=jax.ShapeDtypeStruct((2, depths // 2, rows, columns), jnp.bfloat16),
         scratch_shapes=[pltpu.VMEM((depths * rows, 128), jnp.float32)],
-        compiler_params=pltpu.CompilerParams(vmem_limit_bytes=60 << 20),
+        compiler_params=pltpu.CompilerParams(vmem_limit_bytes=48 << 20),
         cost_estimate=pl.CostEstimate(flops=2 * depths * total * rows * columns, bytes_accessed=14 << 20, transcendentals=0),
         name="fdf",
     )(kt, res.reshape(count, 2, tiles, rows // 2, total, 128))
@@ -446,16 +446,13 @@
         return 0
 
     lax.fori_loop(0, chunks, step, 0)
+    relay(chunks - 2)
+    send_results(16, 24)
     fit_some((me,), halfway, chunks)
-    send_results(16, 24)
-    relay(chunks - 2)
-    fit_some((left, right), halfway, chunks - 1)
-    send_results(24, 28)
     relay(chunks - 1)
-    send_results(28, skies)
-    fit_far(halfway, chunks - 1)
-    fit_some((left, right), chunks - 1, chunks)
-    fit_far(chunks - 1, chunks)
+    send_results(24, skies)
+    fit_some((left, right), halfway, chunks)
+    fit_far(halfway, chunks)
     fill_slots(1, last_ref)
 
     for tile in range(tiles):
@@ -539,7 +536,7 @@
         compiler_params=pltpu.CompilerParams(collective_id=0, has_side_effects=True, vmem_limit_bytes=60 << 20),
         cost_estimate=pl.CostEstimate(flops=6 << 32, bytes_accessed=24 << 20, transcendentals=0),
         name="islands",
-    )(stokes, lam2.reshape(1, chans), peaks, owners, weights)
+    )(stokes, lam2, peaks, owners, weights)
 
 
 def shards(stokes, lam2, peaks, island_owner, fit_matrix):

time: 97.7 us -> 96.3 us (0.986)
  local copies, waits for them, and re-layouts: 1.25 us -> 3.65 us
  waiting for transfers between devices: 3.48 us -> 1.57 us
  Pallas kernels: 84.1 us -> 82.4 us
    unnamed x2 -> x6, local copies, waits for them, and re-layouts: 0.01 us -> 3.65 us
    all_to_all x1, waiting for transfers between devices: 3.48 us -> 1.57 us  [shards(): late = lax.all_to_all(late, 'sky', split_axis=0, concat_axis=0, tiled=True)]
    pallas_call x1, Pallas kernels: 13.4 us -> 11.7 us  [fdf(): pl.pallas_call(fdf_kernel, grid=(count * tiles,), in_specs=[pl.BlockSpec(...]
    reshape x1 -> x0, local copies, waits for them, and re-layouts: 1.25 us -> none  [islands(): lam2.reshape(1, chans)]
  transfers between devices with their start and end apart: 1 -> 1, of which waited for: 1 -> 1; matrix products, arithmetic and copies ran while one was open for 0% -> 0% of each run, Pallas kernels for 14% -> 12%
where the time goes in v6:
time: 96.3 us; the launch traced here: 96 us
  Pallas kernels  82.4 us (86%)
  starting transfers between devices  5.15 us (5%)
  local copies, waits for them, and re-layouts  3.65 us (4%)
  other arithmetic  2.54 us (3%)
  waiting for transfers between devices  1.57 us (2%)
    pallas_call x1, Pallas kernels, islands(): pl.pallas_call(functools.partial(island_kernel, chans), in_specs=[hbm, vm...  70.7 us
    pallas_call x1, Pallas kernels, fdf(): pl.pallas_call(fdf_kernel, grid=(count * tiles,), in_specs=[pl.BlockSpec(...  11.7 us
    all_to_all x1, starting transfers between devices, shards(): late = lax.all_to_all(late, 'sky', split_axis=0, concat_axis=0, tiled=True)  5.15 us
    unnamed x6, local copies, waits for them, and re-layouts  3.65 us
    convert_element_type x1, other arithmetic, shards(): coefficients.astype(jnp.float32)[None]  2.54 us
  transfers between devices with their start and end apart: 1, of which 1 were waited for; matrix products, arithmetic and copies ran while one was open for 0% of the time, Pallas kernels for 12%

profile of v6, /device:TPU:1, one launch (start us, length us, event | category | flops | bytes accessed | tf_op | source)
XLA Modules:
  0.0 96.0 jit_solution(3023815278943275982)
XLA Ops:
  0.6 70.7 %islands.1 = (bf16[4,8,576,128]{3,2,1,0:T(8,128)(2,1)}, bf16[1024,576]{1,0:T(8,128)(2,1)}, bf16[32,2,64,128]{3,2,1,0:T(8,128)(2,1)}, bf16[32,2,64,128]{3,2,1,0:T(8,128)(2,1)}) custom-call(bf16[2,72,4,1024]{3,2,1,0:T(4,128)(2,1)} %stokes_ref.1, f32[288]{0:T(512)} %row_ref.1, s32[8,4,1024]{2,1,0:T(4,128)} %peaks_ref.1, s32[32]{0:T(128)} %bitcast.7, ...), custom_call_target="tpu_custom_call" | custom-call | flops 25769803776 | bytes 25165824 | tf_op jit(solution)/shard_map/islands/pallas_call | solution.py:500
  71.3 5.2 %all-to-all-start = ((bf16[32,2,64,128]{3,2,1,0:T(8,128)(2,1)}), bf16[32,2,64,128]{3,2,1,0:T(8,128)(2,1)S(1)}, u32[]{:S(2)}, u32[]{:S(2)}) async-start(bf16[32,2,64,128]{3,2,1,0:T(8,128)(2,1)} %get-tuple-element.9), calls=%async_computation | async-start | bytes 2097152 | tf_op jit(solution)/shard_map/all_to_all | solution.py:545
  76.5 0.0 copy-start
  76.5 2.3 %copy-done = bf16[4,8,576,128]{3,2,1,0:T(8,128)(2,1)S(1)} copy-done((bf16[4,8,576,128]{3,2,1,0:T(8,128)(2,1)S(1)}, bf16[4,8,576,128]{3,2,1,0:T(8,128)(2,1)}, u32[]{:S(2)}) %copy-start) | copy-done | bytes 4718616
  78.8 0.0 copy-start.1
  78.8 1.3 %copy-done.1 = bf16[1024,576]{1,0:T(8,128)(2,1)S(1)} copy-done((bf16[1024,576]{1,0:T(8,128)(2,1)S(1)}, bf16[1024,576]{1,0:T(8,128)(2,1)}, u32[]{:S(2)}) %copy-start.1) | copy-done | bytes 1179672
  80.1 0.0 copy-start.2
  80.1 11.7 %fdf.1 = bf16[2,512,4,1024]{3,2,1,0:T(4,128)(2,1)} custom-call(bf16[1024,576]{1,0:T(8,128)(2,1)S(1)} %copy-done.1, bf16[4,2,2,2,576,128]{5,4,3,2,1,0:T(8,128)(2,1)S(1)} %bitcast.4), custom_call_target="tpu_custom_call" | custom-call | flops 4831838208 | bytes 14680064 | tf_op jit(solution)/shard_map/fdf/pallas_call | solution.py:100
  91.8 1.6 %all-to-all-done = bf16[32,2,64,128]{3,2,1,0:T(8,128)(2,1)S(1)} async-done(((bf16[32,2,64,128]{3,2,1,0:T(8,128)(2,1)}), bf16[32,2,64,128]{3,2,1,0:T(8,128)(2,1)S(1)}, u32[]{:S(2)}, u32[]{:S(2)}) %all-to-all-start) | async-done | bytes 1048608 | tf_op jit(solution)/shard_map/all_to_all | solution.py:545
  93.4 0.0 copy-done.2
  93.4 2.5 %maximum_convert_fusion = f32[1,32,2,128,128]{4,3,2,1,0:T(8,128)} fusion(bf16[1,32,2,64,128]{4,3,2,1,0:T(8,128)(2,1)S(1)} %bitcast.5, bf16[1,32,2,64,128]{4,3,2,1,0:T(8,128)(2,1)S(1)} %bitcast.6), kind=kLoop, calls=%fused_computation | loop fusion | flops 4194304 | bytes 6291456 | tf_op jit(solution)/shard_map/convert_element_type | solution.py:547
Async XLA Ops:
  71.3 22.1 %all-to-all-start = ((bf16[32,2,64,128]{3,2,1,0:T(8,128)(2,1)}), bf16[32,2,64,128]{3,2,1,0:T(8,128)(2,1)S(1)}, u32[]{:S(2)}, u32[]{:S(2)}) async-start(bf16[32,2,64,128]{3,2,1,0:T(8,128)(2,1)} %get-tuple-element.9), calls=%async_computation | async-start | bytes 2097152 | tf_op jit(solution)/shard_map/all_to_all | solution.py:545
  76.5 2.3 %copy-start = (bf16[4,8,576,128]{3,2,1,0:T(8,128)(2,1)S(1)}, bf16[4,8,576,128]{3,2,1,0:T(8,128)(2,1)}, u32[]{:S(2)}) copy-start(bf16[4,8,576,128]{3,2,1,0:T(8,128)(2,1)} %get-tuple-element.7) | copy-start | bytes 14155780
  78.8 1.3 %copy-start.1 = (bf16[1024,576]{1,0:T(8,128)(2,1)S(1)}, bf16[1024,576]{1,0:T(8,128)(2,1)}, u32[]{:S(2)}) copy-start(bf16[1024,576]{1,0:T(8,128)(2,1)} %get-tuple-element.6.k_ref) | copy-start | bytes 3538948
  80.1 13.3 %copy-start.2 = (bf16[32,2,64,128]{3,2,1,0:T(8,128)(2,1)S(1)}, bf16[32,2,64,128]{3,2,1,0:T(8,128)(2,1)}, u32[]{:S(2)}) copy-start(bf16[32,2,64,128]{3,2,1,0:T(8,128)(2,1)} %get-tuple-element.8) | copy-start | bytes 3145732

commit v7 on v6

--- a/solution.py
+++ b/solution.py
@@ -255,7 +255,7 @@
 
     for tile in range(tiles):
         kept(tile).start()
-        for k in (1, 3, 2):
+        for k in (2, 1, 3):
             part(tile, k).start()
     mine = pl.ds(pl.multiple_of(me * (tiles * 128), 128), tiles * 128)
     pltpu.make_async_copy(peaks_ref.at[:, :, mine], peaks, op).start()

time: 96.3 us -> 96 us (level)
  no operation moved by 1% of the time
where the time goes in v7:
time: 96 us; the launch traced here: 95.7 us
  Pallas kernels  82.4 us (86%)
  starting transfers between devices  4.84 us (5%)
  local copies, waits for them, and re-layouts  3.65 us (4%)
  other arithmetic  2.54 us (3%)
  waiting for transfers between devices  1.57 us (2%)
    pallas_call x1, Pallas kernels, islands(): pl.pallas_call(functools.partial(island_kernel, chans), in_specs=[hbm, vm...  70.8 us
    pallas_call x1, Pallas kernels, fdf(): pl.pallas_call(fdf_kernel, grid=(count * tiles,), in_specs=[pl.BlockSpec(...  11.7 us
    all_to_all x1, starting transfers between devices, shards(): late = lax.all_to_all(late, 'sky', split_axis=0, concat_axis=0, tiled=True)  4.84 us
    unnamed x6, local copies, waits for them, and re-layouts  3.65 us
    convert_element_type x1, other arithmetic, shards(): coefficients.astype(jnp.float32)[None]  2.54 us
  transfers between devices with their start and end apart: 1, of which 1 were waited for; matrix products, arithmetic and copies ran while one was open for 0% of the time, Pallas kernels for 12%

profile of v7, /device:TPU:1, one launch (start us, length us, event | category | flops | bytes accessed | tf_op | source)
XLA Modules:
  0.0 95.7 jit_solution(14710959799079403911)
XLA Ops:
  0.6 70.8 %islands.1 = (bf16[4,8,576,128]{3,2,1,0:T(8,128)(2,1)}, bf16[1024,576]{1,0:T(8,128)(2,1)}, bf16[32,2,64,128]{3,2,1,0:T(8,128)(2,1)}, bf16[32,2,64,128]{3,2,1,0:T(8,128)(2,1)}) custom-call(bf16[2,72,4,1024]{3,2,1,0:T(4,128)(2,1)} %stokes_ref.1, f32[288]{0:T(512)} %row_ref.1, s32[8,4,1024]{2,1,0:T(4,128)} %peaks_ref.1, s32[32]{0:T(128)} %bitcast.7, ...), custom_call_target="tpu_custom_call" | custom-call | flops 25769803776 | bytes 25165824 | tf_op jit(solution)/shard_map/islands/pallas_call | solution.py:500
  71.4 4.8 %all-to-all-start = ((bf16[32,2,64,128]{3,2,1,0:T(8,128)(2,1)}), bf16[32,2,64,128]{3,2,1,0:T(8,128)(2,1)S(1)}, u32[]{:S(2)}, u32[]{:S(2)}) async-start(bf16[32,2,64,128]{3,2,1,0:T(8,128)(2,1)} %get-tuple-element.9), calls=%async_computation | async-start | bytes 2097152 | tf_op jit(solution)/shard_map/all_to_all | solution.py:545
  76.2 0.0 copy-start
  76.3 2.3 %copy-done = bf16[4,8,576,128]{3,2,1,0:T(8,128)(2,1)S(1)} copy-done((bf16[4,8,576,128]{3,2,1,0:T(8,128)(2,1)S(1)}, bf16[4,8,576,128]{3,2,1,0:T(8,128)(2,1)}, u32[]{:S(2)}) %copy-start) | copy-done | bytes 4718616
  78.6 0.0 copy-start.1
  78.6 1.3 %copy-done.1 = bf16[1024,576]{1,0:T(8,128)(2,1)S(1)} copy-done((bf16[1024,576]{1,0:T(8,128)(2,1)S(1)}, bf16[1024,576]{1,0:T(8,128)(2,1)}, u32[]{:S(2)}) %copy-start.1) | copy-done | bytes 1179672
  79.9 0.0 copy-start.2
  79.9 11.7 %fdf.1 = bf16[2,512,4,1024]{3,2,1,0:T(4,128)(2,1)} custom-call(bf16[1024,576]{1,0:T(8,128)(2,1)S(1)} %copy-done.1, bf16[4,2,2,2,576,128]{5,4,3,2,1,0:T(8,128)(2,1)S(1)} %bitcast.4), custom_call_target="tpu_custom_call" | custom-call | flops 4831838208 | bytes 14680064 | tf_op jit(solution)/shard_map/fdf/pallas_call | solution.py:100
  91.6 1.6 %all-to-all-done = bf16[32,2,64,128]{3,2,1,0:T(8,128)(2,1)S(1)} async-done(((bf16[32,2,64,128]{3,2,1,0:T(8,128)(2,1)}), bf16[32,2,64,128]{3,2,1,0:T(8,128)(2,1)S(1)}, u32[]{:S(2)}, u32[]{:S(2)}) %all-to-all-start) | async-done | bytes 1048608 | tf_op jit(solution)/shard_map/all_to_all | solution.py:545
  93.2 0.0 copy-done.2
  93.2 2.5 %maximum_convert_fusion = f32[1,32,2,128,128]{4,3,2,1,0:T(8,128)} fusion(bf16[1,32,2,64,128]{4,3,2,1,0:T(8,128)(2,1)S(1)} %bitcast.5, bf16[1,32,2,64,128]{4,3,2,1,0:T(8,128)(2,1)S(1)} %bitcast.6), kind=kLoop, calls=%fused_computation | loop fusion | flops 4194304 | bytes 6291456 | tf_op jit(solution)/shard_map/convert_element_type | solution.py:547
Async XLA Ops:
  71.4 21.8 %all-to-all-start = ((bf16[32,2,64,128]{3,2,1,0:T(8,128)(2,1)}), bf16[32,2,64,128]{3,2,1,0:T(8,128)(2,1)S(1)}, u32[]{:S(2)}, u32[]{:S(2)}) async-start(bf16[32,2,64,128]{3,2,1,0:T(8,128)(2,1)} %get-tuple-element.9), calls=%async_computation | async-start | bytes 2097152 | tf_op jit(solution)/shard_map/all_to_all | solution.py:545
  76.2 2.3 %copy-start = (bf16[4,8,576,128]{3,2,1,0:T(8,128)(2,1)S(1)}, bf16[4,8,576,128]{3,2,1,0:T(8,128)(2,1)}, u32[]{:S(2)}) copy-start(bf16[4,8,576,128]{3,2,1,0:T(8,128)(2,1)} %get-tuple-element.7) | copy-start | bytes 14155780
  78.6 1.3 %copy-start.1 = (bf16[1024,576]{1,0:T(8,128)(2,1)S(1)}, bf16[1024,576]{1,0:T(8,128)(2,1)}, u32[]{:S(2)}) copy-start(bf16[1024,576]{1,0:T(8,128)(2,1)} %get-tuple-element.6.k_ref) | copy-start | bytes 3538948
  79.9 13.3 %copy-start.2 = (bf16[32,2,64,128]{3,2,1,0:T(8,128)(2,1)S(1)}, bf16[32,2,64,128]{3,2,1,0:T(8,128)(2,1)}, u32[]{:S(2)}) copy-start(bf16[32,2,64,128]{3,2,1,0:T(8,128)(2,1)} %get-tuple-element.8) | copy-start | bytes 3145732
